TPU v7x, 32 devices: a whole 2x2x4 slice. The times are simulated.
32 devices in a mesh: dp: 4 (over y, x), fsdp: 8 (over z, core).
Axes of the slice: x: 2, y: 2, z: 4, core: 2. Of those that a mesh axis runs over, the one named last changes fastest.
Arguments:
- tokens: bfloat16 [32768, 512], P(('dp', 'fsdp')), may hold values from -6 to 6
- memory: bfloat16 [32768, 512], P(('dp', 'fsdp')), may hold values from -6 to 6
- out_cotangent: bfloat16 [32768, 512], P(('dp', 'fsdp')), may hold values from -6 to 6
- seq_lengths: int32 [32, 32], P(('dp', 'fsdp')), may hold values from 0 to 1024, as said below
- memory_lengths: int32 [32, 32], P(('dp', 'fsdp')), may hold values from 0 to 1024, as said below
- residual_gate: float32 [1], replicated, may hold values from 0.5 to 1
- self_in: float32 [512, 1536], P(('dp', 'fsdp')), may hold values from -0.25 to 0.25
- self_out: float32 [512, 512], P(None, ('dp', 'fsdp')), may hold values from -1 to 1
- self_bias: float32 [3, 512], P(None, ('dp', 'fsdp')), may hold values from -1.5 to 1.5
- cross_query: float32 [512, 512], P(('dp', 'fsdp')), may hold values from -0.25 to 0.25
- cross_key_value: float32 [512, 1024], P(('dp', 'fsdp')), may hold values from -0.25 to 0.25
- cross_out: float32 [512, 512], P(None, ('dp', 'fsdp')), may hold values from -1 to 1
- cross_bias: float32 [3, 512], P(None, ('dp', 'fsdp')), may hold values from -1.5 to 1.5
- feed_in: float32 [512, 2048], P(('dp', 'fsdp')), may hold values from -0.25 to 0.25
- feed_out: float32 [2048, 512], P(None, ('dp', 'fsdp')), may hold values from -0.25 to 0.25
- feed_bias_in: float32 [2048], P(('dp', 'fsdp')), may hold values from -2.5 to 2.5
- feed_bias_out: float32 [512], P(('dp', 'fsdp')), may hold values from -6 to 6
Outputs:
- output: bfloat16 [32768, 512], P(('dp', 'fsdp'))
- tokens_grad: float32 [32768, 512], P(('dp', 'fsdp'))
- memory_grad: float32 [32768, 512], P(('dp', 'fsdp'))
- self_in_grad: float32 [512, 1536], P(('dp', 'fsdp'))
- self_out_grad: float32 [512, 512], P(None, ('dp', 'fsdp'))
- self_bias_grad: float32 [3, 512], P(None, ('dp', 'fsdp'))
- cross_query_grad: float32 [512, 512], P(('dp', 'fsdp'))
- cross_key_value_grad: float32 [512, 1024], P(('dp', 'fsdp'))
- cross_out_grad: float32 [512, 512], P(None, ('dp', 'fsdp'))
- cross_bias_grad: float32 [3, 512], P(None, ('dp', 'fsdp'))
- feed_in_grad: float32 [512, 2048], P(('dp', 'fsdp'))
- feed_out_grad: float32 [2048, 512], P(None, ('dp', 'fsdp'))
- feed_bias_in_grad: float32 [2048], P(('dp', 'fsdp'))
- feed_bias_out_grad: float32 [512], P(('dp', 'fsdp'))
Inputs may be any that keep to these rules, and one draw needn't show every extreme that they name: `seq_lengths`: in each row the first k entries (k from 1 to 32, varying by row) are sentence lengths of 1 or more and the rest are 0; a row sums to at most 1024, and the first row holds one sentence of 1024 tokens. `memory_lengths`: nonzero exactly where seq_lengths is; a row sums to at most 1024, and the first row holds one memory of 1024 tokens.
All inputs are finite; a program needn't handle non-finite values.
Results may differ from a plain program's by a relative error of at most 0.023.
The roundings to bfloat16 on the way count: a program that leaves them out, or rounds other values in their place, can miss the bound.
Values may be sent and summed in bfloat16 or wider, within the bound.
No kernel may reach another device: no remote copies, remote signals or barrier semaphores. Data moves between devices by JAX's collectives and lax.ppermute only.
A program may use at most 192 MiB of HBM per device.

v0:
```python
import jax
import jax.numpy as jnp
from jax import lax
from jax.sharding import PartitionSpec as P

HEAD = 64


def segment_numbers(lengths, positions, padding_id):
    boundary = jnp.cumsum(lengths, dtype=jnp.int32)
    position = lax.broadcasted_iota(jnp.int32, (positions, 1), 0)
    number = jnp.sum((position >= boundary[None, :]).astype(jnp.int32), axis=1, dtype=jnp.int32)
    present = position[:, 0] < boundary[-1]
    return (jnp.where(present, number, padding_id), present)


def allowed_block(query_ids, key_ids, row_start, causal):
    allowed = query_ids[:, None] == key_ids[None, :]
    if causal:
        query_place = row_start + lax.broadcasted_iota(jnp.int32, (query_ids.shape[0], 1), 0)
        key_place = lax.broadcasted_iota(jnp.int32, (1, key_ids.shape[0]), 1)
        allowed = allowed & (key_place <= query_place)
    return allowed


def block_layout(queries, query_ids):
    query_count = queries.shape[0]
    block_rows = min(512, query_count)
    block_count = query_count // block_rows
    head_count = queries.shape[1] // HEAD
    shaped = queries.reshape(block_count, block_rows, head_count, HEAD)
    id_blocks = query_ids.reshape(block_count, block_rows)
    starts = jnp.arange(block_count, dtype=jnp.int32) * block_rows
    return (shaped, id_blocks, starts)


def block_scores(query_block, key_heads, id_block, key_ids, row_start, causal):
    raw_scores = jnp.einsum(
        "qhd,khd->hqk", query_block, key_heads, preferred_element_type=jnp.float32
    )
    allowed = allowed_block(id_block, key_ids, row_start, causal)
    return jnp.where(allowed[None], raw_scores * HEAD ** (-0.5), -1e30)


def attend_forward(queries, key_rows, value_rows, query_ids, key_ids, causal):
    shaped, id_blocks, starts = block_layout(queries, query_ids)
    head_count = shaped.shape[2]
    key_heads = key_rows.reshape(key_rows.shape[0], head_count, HEAD)
    value_heads = value_rows.reshape(value_rows.shape[0], head_count, HEAD)

    def per_block(pieces):
        query_block, id_block, row_start = pieces
        scores = block_scores(query_block, key_heads, id_block, key_ids, row_start, causal)
        row_max = jnp.max(scores, axis=-1, keepdims=True)
        exponentials = jnp.exp(scores - row_max)
        row_total = jnp.sum(exponentials, axis=-1, keepdims=True)
        weights_low = (exponentials / row_total).astype(jnp.bfloat16)
        mixed_heads = jnp.einsum(
            "hqk,khd->qhd", weights_low, value_heads, preferred_element_type=jnp.float32
        )
        return (mixed_heads.astype(jnp.bfloat16), (row_max + jnp.log(row_total))[..., 0])

    mixed_heads, log_totals = lax.map(per_block, (shaped, id_blocks, starts))
    return (mixed_heads.reshape(queries.shape[0], queries.shape[1]), log_totals)


def attend_backward(
    queries, key_rows, value_rows, query_ids, key_ids, causal, log_totals, incoming
):
    shaped, id_blocks, starts = block_layout(queries, query_ids)
    head_count = shaped.shape[2]
    key_heads = key_rows.reshape(key_rows.shape[0], head_count, HEAD)
    value_heads = value_rows.reshape(value_rows.shape[0], head_count, HEAD)
    incoming_blocks = incoming.reshape(shaped.shape)

    def per_block(running, pieces):
        key_sum, value_sum = running
        query_block, incoming_block, log_block, id_block, row_start = pieces
        scores = block_scores(query_block, key_heads, id_block, key_ids, row_start, causal)
        chances = jnp.exp(scores - log_block[..., None])
        pushed = jnp.einsum(
            "qhd,khd->hqk", incoming_block, value_heads, preferred_element_type=jnp.float32
        )
        row_delta = jnp.sum(chances * pushed, axis=-1, keepdims=True)
        score_grad = (chances * (pushed - row_delta) * HEAD ** (-0.5)).astype(jnp.bfloat16)
        query_grad = jnp.einsum(
            "hqk,khd->qhd", score_grad, key_heads, preferred_element_type=jnp.float32
        )
        key_sum = key_sum + jnp.einsum(
            "hqk,qhd->khd", score_grad, query_block, preferred_element_type=jnp.float32
        )
        value_sum = value_sum + jnp.einsum(
            "hqk,qhd->khd",
            chances.astype(jnp.bfloat16),
            incoming_block,
            preferred_element_type=jnp.float32,
        )
        return ((key_sum, value_sum), query_grad)

    start_sums = (
        jnp.zeros(key_heads.shape, jnp.float32),
        jnp.zeros(value_heads.shape, jnp.float32),
    )
    sums_after, query_grads = lax.scan(
        per_block, start_sums, (shaped, incoming_blocks, log_totals, id_blocks, starts)
    )
    return (
        query_grads.reshape(queries.shape[0], queries.shape[1]),
        sums_after[0].reshape(key_rows.shape[0], key_rows.shape[1]),
        sums_after[1].reshape(value_rows.shape[0], value_rows.shape[1]),
    )


def gelu_tanh(values):
    return jax.nn.gelu(values, approximate=True)


def on_device(
    tokens,
    memory,
    out_cotangent,
    seq_lengths,
    memory_lengths,
    residual_gate,
    self_in,
    self_out,
    self_bias,
    cross_query,
    cross_key_value,
    cross_out,
    cross_bias,
    feed_in,
    feed_out,
    feed_bias_in,
    feed_bias_out,
):
    low_type = jnp.bfloat16
    full_type = jnp.float32
    model_width = tokens.shape[1]
    slot_count = seq_lengths.shape[1]
    query_ids, present = segment_numbers(seq_lengths[0], tokens.shape[0], slot_count)
    memory_ids = segment_numbers(memory_lengths[0], memory.shape[0], slot_count + 1)[0]
    branch_scale = residual_gate[0] * present.astype(full_type)[:, None]
    zero_row = jnp.zeros((1, model_width), full_type)
    self_full = (
        lax.all_gather(self_in.astype(low_type), ("dp", "fsdp"), axis=0, tiled=True),
        lax.all_gather(self_out.astype(low_type), ("dp", "fsdp"), axis=1, tiled=True),
        lax.all_gather(self_bias.astype(low_type), ("dp", "fsdp"), axis=1, tiled=True),
    )
    self_bias_full = self_full[2].astype(full_type)
    projected = (
        jnp.dot(tokens, self_full[0], preferred_element_type=full_type)
        + jnp.concatenate([self_bias_full[0:1], zero_row, self_bias_full[1:2]], axis=1)
    ).astype(low_type)
    self_mixed, self_logs = attend_forward(
        projected[:, :model_width],
        projected[:, model_width : 2 * model_width],
        projected[:, 2 * model_width :],
        query_ids,
        query_ids,
        True,
    )
    first_sum = tokens.astype(full_type) + branch_scale * (
        jnp.dot(self_mixed, self_full[1], preferred_element_type=full_type) + self_bias_full[2]
    )
    first_low = first_sum.astype(low_type)
    cross_full = (
        lax.all_gather(cross_query.astype(low_type), ("dp", "fsdp"), axis=0, tiled=True),
        lax.all_gather(cross_key_value.astype(low_type), ("dp", "fsdp"), axis=0, tiled=True),
        lax.all_gather(cross_out.astype(low_type), ("dp", "fsdp"), axis=1, tiled=True),
        lax.all_gather(cross_bias.astype(low_type), ("dp", "fsdp"), axis=1, tiled=True),
    )
    cross_bias_full = cross_full[3].astype(full_type)
    cross_queries = (
        jnp.dot(first_low, cross_full[0], preferred_element_type=full_type) + cross_bias_full[0]
    ).astype(low_type)
    memory_kv = (
        jnp.dot(memory, cross_full[1], preferred_element_type=full_type)
        + jnp.concatenate([zero_row, cross_bias_full[1:2]], axis=1)
    ).astype(low_type)
    cross_mixed, cross_logs = attend_forward(
        cross_queries,
        memory_kv[:, :model_width],
        memory_kv[:, model_width:],
        query_ids,
        memory_ids,
        False,
    )
    second_sum = first_sum + branch_scale * (
        jnp.dot(cross_mixed, cross_full[2], preferred_element_type=full_type) + cross_bias_full[2]
    )
    second_low = second_sum.astype(low_type)
    feed_full = (
        lax.all_gather(feed_in.astype(low_type), ("dp", "fsdp"), axis=0, tiled=True),
        lax.all_gather(feed_out.astype(low_type), ("dp", "fsdp"), axis=1, tiled=True),
        lax.all_gather(feed_bias_in.astype(low_type), ("dp", "fsdp"), axis=0, tiled=True),
        lax.all_gather(feed_bias_out.astype(low_type), ("dp", "fsdp"), axis=0, tiled=True),
    )
    before = jnp.dot(second_low, feed_full[0], preferred_element_type=full_type) + feed_full[
        2
    ].astype(full_type)
    hidden = gelu_tanh(before).astype(low_type)
    output = (
        second_sum
        + branch_scale
        * (
            jnp.dot(hidden, feed_full[1], preferred_element_type=full_type)
            + feed_full[3].astype(full_type)
        )
    ).astype(low_type)
    feed_back = (
        lax.all_gather(feed_in.astype(low_type), ("dp", "fsdp"), axis=0, tiled=True),
        lax.all_gather(feed_out.astype(low_type), ("dp", "fsdp"), axis=1, tiled=True),
    )
    upstream = out_cotangent.astype(full_type)
    feed_signal = (branch_scale * upstream).astype(low_type)
    feed_out_local = jnp.einsum("tf,td->fd", hidden, feed_signal, preferred_element_type=full_type)
    feed_bias_out_local = jnp.sum(feed_signal.astype(full_type), axis=0)
    hidden_grad = jnp.einsum(
        "td,fd->tf", feed_signal, feed_back[1], preferred_element_type=full_type
    )
    gelu_pull = jax.vjp(gelu_tanh, before)[1]
    before_grad = gelu_pull(hidden_grad)[0].astype(low_type)
    feed_in_local = jnp.einsum(
        "td,tf->df", second_low, before_grad, preferred_element_type=full_type
    )
    feed_bias_in_local = jnp.sum(before_grad.astype(full_type), axis=0)
    second_grad = upstream + jnp.einsum(
        "tf,df->td", before_grad, feed_back[0], preferred_element_type=full_type
    )
    feed_owned = (
        lax.psum_scatter(feed_in_local, ("dp", "fsdp"), scatter_dimension=0, tiled=True),
        lax.psum_scatter(feed_out_local, ("dp", "fsdp"), scatter_dimension=1, tiled=True),
        lax.psum_scatter(feed_bias_in_local, ("dp", "fsdp"), scatter_dimension=0, tiled=True),
        lax.psum_scatter(feed_bias_out_local, ("dp", "fsdp"), scatter_dimension=0, tiled=True),
    )
    cross_back = (
        lax.all_gather(cross_query.astype(low_type), ("dp", "fsdp"), axis=0, tiled=True),
        lax.all_gather(cross_key_value.astype(low_type), ("dp", "fsdp"), axis=0, tiled=True),
        lax.all_gather(cross_out.astype(low_type), ("dp", "fsdp"), axis=1, tiled=True),
    )
    cross_signal = (branch_scale * second_grad).astype(low_type)
    cross_out_local = jnp.einsum(
        "tc,td->cd", cross_mixed, cross_signal, preferred_element_type=full_type
    )
    cross_mixed_grad = jnp.einsum(
        "td,cd->tc", cross_signal, cross_back[2], preferred_element_type=full_type
    ).astype(low_type)
    query_part, key_part, value_part = attend_backward(
        cross_queries,
        memory_kv[:, :model_width],
        memory_kv[:, model_width:],
        query_ids,
        memory_ids,
        False,
        cross_logs,
        cross_mixed_grad,
    )
    cross_query_signal = query_part.astype(low_type)
    memory_signal = jnp.concatenate([key_part, value_part], axis=1).astype(low_type)
    cross_query_local = jnp.einsum(
        "tc,td->cd", first_low, cross_query_signal, preferred_element_type=full_type
    )
    cross_key_value_local = jnp.einsum(
        "mc,me->ce", memory, memory_signal, preferred_element_type=full_type
    )
    cross_bias_local = jnp.stack(
        [
            jnp.sum(cross_query_signal.astype(full_type), axis=0),
            jnp.sum(memory_signal[:, model_width:].astype(full_type), axis=0),
            jnp.sum(cross_signal.astype(full_type), axis=0),
        ]
    )
    memory_grad = jnp.einsum(
        "me,ce->mc", memory_signal, cross_back[1], preferred_element_type=full_type
    )
    first_grad = second_grad + jnp.einsum(
        "td,cd->tc", cross_query_signal, cross_back[0], preferred_element_type=full_type
    )
    cross_owned = (
        lax.psum_scatter(cross_query_local, ("dp", "fsdp"), scatter_dimension=0, tiled=True),
        lax.psum_scatter(cross_key_value_local, ("dp", "fsdp"), scatter_dimension=0, tiled=True),
        lax.psum_scatter(cross_out_local, ("dp", "fsdp"), scatter_dimension=1, tiled=True),
        lax.psum_scatter(cross_bias_local, ("dp", "fsdp"), scatter_dimension=1, tiled=True),
    )
    self_back = (
        lax.all_gather(self_in.astype(low_type), ("dp", "fsdp"), axis=0, tiled=True),
        lax.all_gather(self_out.astype(low_type), ("dp", "fsdp"), axis=1, tiled=True),
    )
    self_signal = (branch_scale * first_grad).astype(low_type)
    self_out_local = jnp.einsum(
        "tc,td->cd", self_mixed, self_signal, preferred_element_type=full_type
    )
    self_mixed_grad = jnp.einsum(
        "td,cd->tc", self_signal, self_back[1], preferred_element_type=full_type
    ).astype(low_type)
    query_self, key_self, value_self = attend_backward(
        projected[:, :model_width],
        projected[:, model_width : 2 * model_width],
        projected[:, 2 * model_width :],
        query_ids,
        query_ids,
        True,
        self_logs,
        self_mixed_grad,
    )
    projected_signal = jnp.concatenate([query_self, key_self, value_self], axis=1).astype(low_type)
    self_in_local = jnp.einsum(
        "tc,te->ce", tokens, projected_signal, preferred_element_type=full_type
    )
    self_bias_local = jnp.stack(
        [
            jnp.sum(projected_signal[:, :model_width].astype(full_type), axis=0),
            jnp.sum(projected_signal[:, 2 * model_width :].astype(full_type), axis=0),
            jnp.sum(self_signal.astype(full_type), axis=0),
        ]
    )
    tokens_grad = first_grad + jnp.einsum(
        "te,ce->tc", projected_signal, self_back[0], preferred_element_type=full_type
    )
    self_owned = (
        lax.psum_scatter(self_in_local, ("dp", "fsdp"), scatter_dimension=0, tiled=True),
        lax.psum_scatter(self_out_local, ("dp", "fsdp"), scatter_dimension=1, tiled=True),
        lax.psum_scatter(self_bias_local, ("dp", "fsdp"), scatter_dimension=1, tiled=True),
    )
    return (
        output,
        tokens_grad,
        memory_grad,
        self_owned[0],
        self_owned[1],
        self_owned[2],
        cross_owned[0],
        cross_owned[1],
        cross_owned[2],
        cross_owned[3],
        feed_owned[0],
        feed_owned[1],
        feed_owned[2],
        feed_owned[3],
    )


def solution(mesh):
    return jax.shard_map(
        on_device,
        mesh=mesh,
        in_specs=(
            P(("dp", "fsdp"), None),
            P(("dp", "fsdp"), None),
            P(("dp", "fsdp"), None),
            P(("dp", "fsdp"), None),
            P(("dp", "fsdp"), None),
            P(),
            P(("dp", "fsdp"), None),
            P(None, ("dp", "fsdp")),
            P(None, ("dp", "fsdp")),
            P(("dp", "fsdp"), None),
            P(("dp", "fsdp"), None),
            P(None, ("dp", "fsdp")),
            P(None, ("dp", "fsdp")),
            P(("dp", "fsdp"), None),
            P(None, ("dp", "fsdp")),
            P(("dp", "fsdp")),
            P(("dp", "fsdp")),
        ),
        out_specs=(
            P(("dp", "fsdp"), None),
            P(("dp", "fsdp"), None),
            P(("dp", "fsdp"), None),
            P(("dp", "fsdp"), None),
            P(None, ("dp", "fsdp")),
            P(None, ("dp", "fsdp")),
            P(("dp", "fsdp"), None),
            P(("dp", "fsdp"), None),
            P(None, ("dp", "fsdp")),
            P(None, ("dp", "fsdp")),
            P(("dp", "fsdp"), None),
            P(None, ("dp", "fsdp")),
            P(("dp", "fsdp")),
            P(("dp", "fsdp")),
        ),
        check_vma=False,
    )
```

profile of v0, /device:TPU:0, one launch (start us, length us, event | category | flops | bytes accessed | tf_op | source)
XLA Modules:
  0.0 1927.4 jit_solution(14092073044912713817)
XLA Ops:
  20.3 42.3 %all-reduce.6 = (bf16[2048]{0:T(1024)(128)(2,1)S(1)}, bf16[512]{0:T(512)(128)(2,1)}) all-reduce(bf16[2048]{0:T(1024)(128)(2,1)S(1)} %dynamic-update-slice, bf16[512]{0:T(512)(128)(2,1)S(1)} %dynamic-update-slice.1), channel_id=1, replica_groups=mesh['dp'=4,'fsdp'=8] {'dp','fsdp'}, use_global_device_ids=true, to_apply=%add.1 | all-reduce | flops 2560 | bytes 10240
  68.3 40.4 %all-gather.1 = bf16[32,16,3]{1,2,0:T(4,128)(2,1)S(1)} all-gather(bf16[1,16,3]{1,2,0:T(4,128)(2,1)S(1)} %convert_bitcast_fusion), channel_id=1, replica_groups=mesh['dp'=4,'fsdp'=8] {'dp','fsdp'}, dimensions={0}, use_global_device_ids=true | all-gather | bytes 3168 | tf_op jit(solution)/shard_map/all_gather | solution.py:171
  108.8 36.7 %all-gather = bf16[32,16,3]{1,2,0:T(4,128)(2,1)S(1)} all-gather(bf16[1,16,3]{1,2,0:T(4,128)(2,1)S(1)} %convert_bitcast_fusion.1), channel_id=1, replica_groups=mesh['dp'=4,'fsdp'=8] {'dp','fsdp'}, dimensions={0}, use_global_device_ids=true | all-gather | bytes 3168 | tf_op jit(solution)/shard_map/all_gather | solution.py:148
  147.1 43.7 %all_gather.46 = bf16[512,512]{0,1:T(8,128)(2,1)} all-gather(bf16[512,16]{0,1:T(8,128)(2,1)S(1)} %convert_element_type.184), channel_id=1, replica_groups=mesh['dp'=4,'fsdp'=8] {'dp','fsdp'}, dimensions={1}, use_global_device_ids=true | all-gather | bytes 540672 | tf_op jit(solution)/shard_map/all_gather | solution.py:170
  190.8 41.7 %all_gather.43 = bf16[512,512]{1,0:T(8,128)(2,1)} all-gather(bf16[16,512]{1,0:T(8,128)(2,1)S(1)} %convert_element_type.178), channel_id=1, replica_groups=mesh['dp'=4,'fsdp'=8] {'dp','fsdp'}, dimensions={0}, use_global_device_ids=true | all-gather | bytes 540672 | tf_op jit(solution)/shard_map/all_gather | solution.py:168
  232.5 43.0 %all_gather.42 = bf16[512,512]{0,1:T(8,128)(2,1)} all-gather(bf16[512,16]{0,1:T(8,128)(2,1)S(1)} %convert_element_type.175), channel_id=1, replica_groups=mesh['dp'=4,'fsdp'=8] {'dp','fsdp'}, dimensions={1}, use_global_device_ids=true | all-gather | bytes 540672 | tf_op jit(solution)/shard_map/all_gather | solution.py:147
  296.3 33.1 %while.54 = (s32[]{:T(128)}, bf16[2,512,8,64]{1,3,2,0:T(8,128)(2,1)}, f32[2,8,512]{2,1,0:T(8,128)S(1)}, s32[2,512]{1,0:T(2,128)S(1)}, s32[1024]{0:T(1024)S(1)}, ...) while((s32[]{:T(128)}, ...), condition=%wide.region_5.6_spmd, body=%wide.region_2.5_spmd.sunk | while | flops 1125904896 | bytes 64108740 | solution.py:63
  341.0 17.1 copy.123
  359.2 30.2 %while.55 = (s32[]{:T(128)}, bf16[2,512,8,64]{1,3,2,0:T(8,128)(2,1)}, f32[2,8,512]{2,1,0:T(8,128)S(1)}, s32[2,512]{1,0:T(2,128)S(1)}, s32[1024]{0:T(1024)S(1)}, ...) while((s32[]{:T(128)}, ...), condition=%wide.region_11.12_spmd, body=%wide.region_8.11_spmd.sunk | while | flops 1124855808 | bytes 64104620 | solution.py:63
  395.5 10.6 multiply_convert_fusion.2
  406.0 11.4 convert_reduce_fusion
  431.9 135.3 %while.56 = (s32[]{:T(128)}, f32[1024,8,64]{0,2,1:T(8,128)}, f32[1024,8,64]{0,2,1:T(8,128)}, bf16[2,512,8,64]{1,3,2,0:T(8,128)(2,1)}, bf16[2,512,8,64]{1,3,2,0:T...) while((s32[]{:T(128)}, f32[1024,8,64]{0,2,1:T(8,128)}, ...), condition=%wide.region_14.15_spmd.clone, body=%wide.region_12.14_spmd.clone.sunk | while | flops 2745706496 | bytes 267446480 | solution.py:104
  453.1 22.7 %fusion.242 = bf16[2,512,8,64]{1,3,2,0:T(8,128)(2,1)} fusion(bf16[2,512,8,64]{1,3,2,0:T(8,128)(2,1)} %get-tuple-element.1022, s32[]{:T(128)S(6)} %copy.185, bf16[1024,8,64]{0,2,1:T(8,128)(2,1)} %get-tuple-element.1039, f32[8,512,1024]{2,1,0:T(8,128)} %copy-done.1, f32[8,512,1024]{2,1,0:T(8,128)} %fusion.241), kind=kOutput, calls=%fused_computation.52.clone.1 | convolution fusion | flops 557847552 | bytes 69206016 | tf_op jit(solution)/shard_map/while/body/eval_jaxpr/hqk,khd->qhd/dot_general | solution.py:86
  475.8 23.4 %bitcast_add_fusion.8 = f32[1024,8,64]{0,2,1:T(8,128)} fusion(f32[1024,8,64]{0,2,1:T(8,128)} %get-tuple-element.1020, f32[8,512,1024]{2,1,0:T(8,128)} %copy-done.1, f32[8,512,1024]{2,1,0:T(8,128)} %fusion.241, pred[]{:T(512)S(6)} %compare.7, bf16[2,512,8,64]{1,3,2,0:T(8,128)(2,1)} %get-tuple-element.1036, s32[]{:T(128)S(6)} %copy.185), kind=kOutput, calls=%fused_computation.50.clone.1 | convolution fusion | flops 558896128 | bytes 71827464 | tf_op jit(solution)/shard_map/while/body/eval_jaxpr/hqk,qhd->khd/dot_general | solution.py:89
  520.5 22.7 %fusion.242 = bf16[2,512,8,64]{1,3,2,0:T(8,128)(2,1)} fusion(bf16[2,512,8,64]{1,3,2,0:T(8,128)(2,1)} %get-tuple-element.1022, s32[]{:T(128)S(6)} %copy.185, bf16[1024,8,64]{0,2,1:T(8,128)(2,1)} %get-tuple-element.1039, f32[8,512,1024]{2,1,0:T(8,128)} %copy-done.1, f32[8,512,1024]{2,1,0:T(8,128)} %fusion.241), kind=kOutput, calls=%fused_computation.52.clone.1 | convolution fusion | flops 557847552 | bytes 69206016 | tf_op jit(solution)/shard_map/while/body/eval_jaxpr/hqk,khd->qhd/dot_general | solution.py:86
  543.2 24.0 %bitcast_add_fusion.8 = f32[1024,8,64]{0,2,1:T(8,128)} fusion(f32[1024,8,64]{0,2,1:T(8,128)} %get-tuple-element.1020, f32[8,512,1024]{2,1,0:T(8,128)} %copy-done.1, f32[8,512,1024]{2,1,0:T(8,128)} %fusion.241, pred[]{:T(512)S(6)} %compare.7, bf16[2,512,8,64]{1,3,2,0:T(8,128)(2,1)} %get-tuple-element.1036, s32[]{:T(128)S(6)} %copy.185), kind=kOutput, calls=%fused_computation.50.clone.1 | convolution fusion | flops 558896128 | bytes 71827464 | tf_op jit(solution)/shard_map/while/body/eval_jaxpr/hqk,qhd->khd/dot_general | solution.py:89
  584.2 138.2 %while.57 = (s32[]{:T(128)}, f32[1024,8,64]{0,2,1:T(8,128)}, f32[1024,8,64]{0,2,1:T(8,128)}, bf16[2,512,8,64]{1,3,2,0:T(8,128)(2,1)}, bf16[2,512,8,64]{1,3,2,0:T...) while((s32[]{:T(128)}, f32[1024,8,64]{0,2,1:T(8,128)}, ...), condition=%wide.region_17.18_spmd.clone, body=%wide.region_15.17_spmd.clone.sunk | while | flops 2746755584 | bytes 267450592 | solution.py:104
  606.5 22.7 %fusion.255 = bf16[2,512,8,64]{1,3,2,0:T(8,128)(2,1)} fusion(bf16[2,512,8,64]{1,3,2,0:T(8,128)(2,1)} %get-tuple-element.1062, s32[]{:T(128)S(6)} %copy.197, bf16[1024,8,64]{0,2,1:T(8,128)(2,1)} %get-tuple-element.1081, f32[8,512,1024]{2,1,0:T(8,128)} %copy-done.2, f32[8,512,1024]{2,1,0:T(8,128)} %fusion.254), kind=kOutput, calls=%fused_computation.89.clone.1 | convolution fusion | flops 557847552 | bytes 69206016 | tf_op jit(solution)/shard_map/while/body/eval_jaxpr/hqk,khd->qhd/dot_general | solution.py:86
  629.2 23.5 %bitcast_add_fusion.10 = f32[1024,8,64]{0,2,1:T(8,128)} fusion(f32[1024,8,64]{0,2,1:T(8,128)} %get-tuple-element.1060, f32[8,512,1024]{2,1,0:T(8,128)} %copy-done.2, f32[8,512,1024]{2,1,0:T(8,128)} %fusion.254, pred[]{:T(512)S(6)} %compare.8, bf16[2,512,8,64]{1,3,2,0:T(8,128)(2,1)} %get-tuple-element.1077, s32[]{:T(128)S(6)} %copy.197), kind=kOutput, calls=%fused_computation.85.clone.1 | convolution fusion | flops 558896128 | bytes 71827464 | tf_op jit(solution)/shard_map/while/body/eval_jaxpr/hqk,qhd->khd/dot_general | solution.py:89
  667.4 8.1 fusion.254
  675.5 22.7 %fusion.255 = bf16[2,512,8,64]{1,3,2,0:T(8,128)(2,1)} fusion(bf16[2,512,8,64]{1,3,2,0:T(8,128)(2,1)} %get-tuple-element.1062, s32[]{:T(128)S(6)} %copy.197, bf16[1024,8,64]{0,2,1:T(8,128)(2,1)} %get-tuple-element.1081, f32[8,512,1024]{2,1,0:T(8,128)} %copy-done.2, f32[8,512,1024]{2,1,0:T(8,128)} %fusion.254), kind=kOutput, calls=%fused_computation.89.clone.1 | convolution fusion | flops 557847552 | bytes 69206016 | tf_op jit(solution)/shard_map/while/body/eval_jaxpr/hqk,khd->qhd/dot_general | solution.py:86
  698.2 24.0 %bitcast_add_fusion.10 = f32[1024,8,64]{0,2,1:T(8,128)} fusion(f32[1024,8,64]{0,2,1:T(8,128)} %get-tuple-element.1060, f32[8,512,1024]{2,1,0:T(8,128)} %copy-done.2, f32[8,512,1024]{2,1,0:T(8,128)} %fusion.254, pred[]{:T(512)S(6)} %compare.8, bf16[2,512,8,64]{1,3,2,0:T(8,128)(2,1)} %get-tuple-element.1077, s32[]{:T(128)S(6)} %copy.197), kind=kOutput, calls=%fused_computation.85.clone.1 | convolution fusion | flops 558896128 | bytes 71827464 | tf_op jit(solution)/shard_map/while/body/eval_jaxpr/hqk,qhd->khd/dot_general | solution.py:89
  775.6 38.2 %all-reduce.5 = (f32[2048]{0:T(1024)S(1)}, f32[512]{0:T(512)S(1)}) all-reduce(f32[2048]{0:T(1024)S(1)} %copy-done.47, f32[512]{0:T(512)S(1)} %copy-done.49), channel_id=11, replica_groups=mesh['dp'=4,'fsdp'=8] {'dp','fsdp'}, use_global_device_ids=true, to_apply=%region_34.35.clone | all-reduce | flops 2560 | bytes 20480
  826.2 34.0 %reduce-scatter.30.cloned.1.call-done = f32[16,3]{1,0:T(8,128)} async-done(((f32[512,3]{1,0:T(8,128)}), f32[16,3]{1,0:T(8,128)}) %reduce-scatter.30.cloned.1.call-update) | async-done | bytes 208
  861.5 130.6 %reduce-scatter.34.cloned.1.call-done = f32[16,3]{1,0:T(8,128)} async-done(((f32[512,3]{1,0:T(8,128)}), f32[16,3]{1,0:T(8,128)}) %reduce-scatter.34.cloned.1.call-update) | async-done | bytes 208
  993.5 132.2 %reduce-scatter.22.cloned.1.call-done = f32[512,16]{0,1:T(8,128)} async-done(((f32[512,512]{0,1:T(8,128)}), f32[512,16]{0,1:T(8,128)}) %reduce-scatter.22.cloned.1.call-update) | async-done | bytes 32784 | tf_op jit(solution)/shard_map/reduce_scatter | solution.py:283
  1125.7 134.1 %reduce-scatter.18.cloned.1.call-done = f32[512,16]{0,1:T(8,128)} async-done(((f32[512,512]{0,1:T(8,128)}), f32[512,16]{0,1:T(8,128)}) %reduce-scatter.18.cloned.1.call-update) | async-done | bytes 32784 | tf_op jit(solution)/shard_map/reduce_scatter | solution.py:323
  1259.7 134.0 %reduce-scatter.20.cloned.1.call-done = f32[16,512]{1,0:T(8,128)} async-done(((f32[512,512]{1,0:T(8,128)}), f32[16,512]{1,0:T(8,128)}) %reduce-scatter.20.cloned.1.call-update) | async-done | bytes 32784 | tf_op jit(solution)/shard_map/reduce_scatter | solution.py:281
  1393.7 104.6 %reduce-scatter.28.cloned.1.call-done = f32[16,1536]{1,0:T(8,128)} async-done(((f32[512,1536]{1,0:T(8,128)}), f32[16,1536]{1,0:T(8,128)}) %reduce-scatter.28.cloned.1.call-update) | async-done | bytes 98320
  1498.3 138.5 %reduce-scatter.32.cloned.1.call-done = f32[16,1024]{1,0:T(8,128)} async-done(((f32[512,1024]{1,0:T(8,128)}), f32[16,1024]{1,0:T(8,128)}) %reduce-scatter.32.cloned.1.call-update) | async-done | bytes 65552
  1636.8 142.0 %reduce-scatter.26.cloned.1.call-done = f32[2048,16]{0,1:T(8,128)} async-done(((f32[2048,512]{0,1:T(8,128)}), f32[2048,16]{0,1:T(8,128)}) %reduce-scatter.26.cloned.1.call-update) | async-done | bytes 131088 | tf_op jit(solution)/shard_map/reduce_scatter | solution.py:233
  1778.8 141.6 %reduce-scatter.24.cloned.1.call-done = f32[16,2048]{1,0:T(8,128)} async-done(((f32[512,2048]{1,0:T(8,128)}), f32[16,2048]{1,0:T(8,128)}) %reduce-scatter.24.cloned.1.call-update) | async-done | bytes 131088 | tf_op jit(solution)/shard_map/reduce_scatter | solution.py:232
  (335 shorter events, 300.3 us)
Async XLA Ops:
  7.2 269.7 %copy-start = (bf16[1024,512]{1,0:T(8,128)(2,1)S(1)}, bf16[1024,512]{1,0:T(8,128)(2,1)}, u32[]{:S(2)}) copy-start(bf16[1024,512]{1,0:T(8,128)(2,1)} %param.26) | copy-start | bytes 3145732
  7.2 269.6 %all-gather.9.cloned.1.call-start = ((), (), s32[]{:S(2)}) async-start(), calls=%async_computation.10 | async-start | bytes 1081344 | tf_op jit(solution)/shard_map/all_gather | solution.py:169
  8.8 272.2 %all-gather.7.cloned.1.call-start = ((), (), s32[]{:S(2)}) async-start(), calls=%async_computation.9 | async-start | bytes 1622016 | tf_op jit(solution)/shard_map/all_gather | solution.py:146
  10.4 385.1 %all-gather.11.cloned.1.call-start = ((), (), s32[]{:S(2)}) async-start(), calls=%async_computation.11 | async-start | bytes 2162688 | tf_op jit(solution)/shard_map/all_gather | solution.py:194
  12.0 394.0 %all-gather.13.cloned.1.call-start = ((), (), s32[]{:S(2)}) async-start(), calls=%async_computation.12 | async-start | bytes 2162688 | tf_op jit(solution)/shard_map/all_gather | solution.py:195
  13.6 846.5 %reduce-scatter.30.cloned.1.call-start = ((), (), s32[]{:S(2)}) async-start(), calls=%async_computation.19 | async-start | bytes 270336
  329.5 5.8 copy-start.24
  329.5 5.8 copy-start.52
  337.0 22.2 %copy-start.5 = (bf16[1024,512]{0,1:T(8,128)(2,1)S(1)}, bf16[1024,512]{0,1:T(8,128)(2,1)}, u32[]{:S(2)}) copy-start(bf16[1024,512]{0,1:T(8,128)(2,1)} %get-tuple-element.682) | copy-start | bytes 3145732
  337.0 22.2 %copy-start.7 = (bf16[1024,512]{0,1:T(8,128)(2,1)S(1)}, bf16[1024,512]{0,1:T(8,128)(2,1)}, u32[]{:S(2)}) copy-start(bf16[1024,512]{0,1:T(8,128)(2,1)} %get-tuple-element.683) | copy-start | bytes 3145732
  337.0 22.2 %copy-start.37 = (s32[1024]{0:T(1024)S(1)}, s32[1024]{0:T(1024)}, u32[]{:S(2)}) copy-start(s32[1024]{0:T(1024)} %fusion.128) | copy-start | bytes 12292
  406.0 11.4 copy-start.55
  406.0 11.4 copy-start.59
  438.7 6.4 copy-start.1
  505.4 6.9 copy-start.1
  571.8 6.0 copy-start.34
  578.4 5.8 copy-start.4
  578.4 5.7 copy-start.36
  592.0 6.4 copy-start.2
  660.4 6.9 copy-start.2
  725.0 19.9 %copy-start.14 = (bf16[64,8,2,512]{3,1,2,0:T(8,128)(2,1)}, bf16[64,8,2,512]{3,1,2,0:T(8,128)(2,1)S(1)}, u32[]{:S(2)}) copy-start(bf16[64,8,2,512]{3,1,2,0:T(8,128)(2,1)S(1)} %copy.154) | copy-start | bytes 3145732
  725.0 6.7 copy-start.46
  725.0 6.7 copy-start.50
  728.9 263.2 %reduce-scatter.34.cloned.1.call-start = ((), (), s32[]{:S(2)}) async-start(), calls=%async_computation.21 | async-start | bytes 270336
  732.6 6.9 copy-start.11
  732.6 393.1 %reduce-scatter.22.cloned.1.call-start = ((), (), s32[]{:S(2)}) async-start(), calls=%async_computation.15 | async-start | bytes 1081344 | tf_op jit(solution)/shard_map/reduce_scatter | solution.py:283
  736.1 523.6 %reduce-scatter.18.cloned.1.call-start = ((), (), s32[]{:S(2)}) async-start(), calls=%async_computation.13 | async-start | bytes 1081344 | tf_op jit(solution)/shard_map/reduce_scatter | solution.py:323
  739.5 654.2 %reduce-scatter.20.cloned.1.call-start = ((), (), s32[]{:S(2)}) async-start(), calls=%async_computation.14 | async-start | bytes 1081344 | tf_op jit(solution)/shard_map/reduce_scatter | solution.py:281
  743.0 755.3 %reduce-scatter.28.cloned.1.call-start = ((), (), s32[]{:S(2)}) async-start(), calls=%async_computation.18 | async-start | bytes 3244032
  754.2 882.6 %reduce-scatter.32.cloned.1.call-start = ((), (), s32[]{:S(2)}) async-start(), calls=%async_computation.20 | async-start | bytes 2162688
  759.8 1019.0 %reduce-scatter.26.cloned.1.call-start = ((), (), s32[]{:S(2)}) async-start(), calls=%async_computation.17 | async-start | bytes 4325376 | tf_op jit(solution)/shard_map/reduce_scatter | solution.py:233
  766.8 1153.7 %reduce-scatter.24.cloned.1.call-start = ((), (), s32[]{:S(2)}) async-start(), calls=%async_computation.16 | async-start | bytes 4325376 | tf_op jit(solution)/shard_map/reduce_scatter | solution.py:232
  (51 other events, 165.0 us)
Sparse Core Ops, SparseCore 0:
  11.6 56.7 all-gather.8
  71.9 54.1 all-gather.6
  129.7 56.2 all-gather.10
  189.3 56.0 all-gather.12
  729.1 131.0 reduce-scatter.29
  862.4 129.7 reduce-scatter.33
  994.9 130.7 reduce-scatter.21
  1128.6 131.1 reduce-scatter.17
  1262.5 131.0 reduce-scatter.19
  1400.4 97.7 reduce-scatter.27
  1501.2 135.5 reduce-scatter.31
  1639.5 139.2 reduce-scatter.25
  1781.6 138.7 reduce-scatter.23
where the time goes:
time: 1930 us
  waiting for transfers between devices  1090 us (56%)
  matrix products  385 us (20%)
  blocking collectives  286 us (15%)
  local copies, waits for them, and re-layouts  98.2 us (5%)
  other arithmetic  48.6 us (3%)
    unnamed x17, waiting for transfers between devices  408 us
    reduce_scatter x1, waiting for transfers between devices, on_device(): lax.psum_scatter(feed_out_local, ('dp', 'fsdp'), scatter_dimension=1, til...  142 us
    reduce_scatter x1, waiting for transfers between devices, on_device(): lax.psum_scatter(feed_in_local, ('dp', 'fsdp'), scatter_dimension=0, tile...  142 us
    reduce_scatter x1, waiting for transfers between devices, on_device(): lax.psum_scatter(self_out_local, ('dp', 'fsdp'), scatter_dimension=1, til...  134 us
    reduce_scatter x1, waiting for transfers between devices, on_device(): lax.psum_scatter(cross_query_local, ('dp', 'fsdp'), scatter_dimension=0,...  134 us
    reduce_scatter x1, waiting for transfers between devices, on_device(): lax.psum_scatter(cross_out_local, ('dp', 'fsdp'), scatter_dimension=1, ti...  132 us
    dot_general x4, matrix products, per_block(): jnp.einsum('hqk,qhd->khd', score_grad, query_block, preferred_element_typ...  94.8 us
    dot_general x4, matrix products, per_block(): jnp.einsum('hqk,khd->qhd', score_grad, key_heads, preferred_element_type=...  90.7 us
  transfers between devices with their start and end apart: 13, of which 9 were waited for; matrix products, arithmetic and copies ran while one was open for 10% of the time, Pallas kernels for 0%

commit v1 on v0

--- a/solution.py
+++ b/solution.py
@@ -4,6 +4,52 @@
 from jax.sharding import PartitionSpec as P
 
 HEAD = 64
+AXES = ("dp", "fsdp")
+
+
+def rows_all(shard):
+    return lax.all_gather(shard, AXES, axis=0, tiled=True)
+
+
+def sum_to_owners(grads, device_count, orders):
+    me = lax.axis_index(AXES)
+    running = []
+    for grad in grads:
+        rows, columns = grad.shape
+        bits = device_count.bit_length() - 1
+        running.append(grad.reshape((2,) * bits + (rows // device_count, columns)))
+    left = [list(range(device_count.bit_length() - 1)) for _ in grads]
+    for step in range(device_count.bit_length() - 1):
+        sent = []
+        for part, order in enumerate(orders):
+            bit = order[step]
+            axis = len(left[part]) - 1 - left[part].index(bit)
+            mine = (me >> bit) & 1
+            away = lax.dynamic_index_in_dim(running[part], 1 - mine, axis, keepdims=False)
+            pairs = [(i, i ^ (1 << bit)) for i in range(device_count)]
+            sent.append((axis, mine, lax.ppermute(away.astype(jnp.bfloat16), AXES, pairs)))
+            left[part].remove(bit)
+        for part, (axis, mine, got) in enumerate(sent):
+            kept = lax.dynamic_index_in_dim(running[part], mine, axis, keepdims=False)
+            running[part] = kept.astype(jnp.float32) + got.astype(jnp.float32)
+    return running
+
+
+def column_orders(device_count):
+    bits = device_count.bit_length() - 1
+    high = list(range(1, bits))[::-1]
+    first = [0] + high
+    second = [0] + [high[1], high[0]] + high[2:]
+    return first, second
+
+
+def scatter_rows(grad, device_count):
+    half = grad.shape[1] // 256 * 128
+    first, second = column_orders(device_count)
+    left, right = sum_to_owners(
+        [grad[:, :half], grad[:, half:]], device_count, (first, second)
+    )
+    return jnp.concatenate([left, right], axis=1)
 
 
 def segment_numbers(lengths, positions, padding_id):
@@ -142,12 +188,43 @@
     memory_ids = segment_numbers(memory_lengths[0], memory.shape[0], slot_count + 1)[0]
     branch_scale = residual_gate[0] * present.astype(full_type)[:, None]
     zero_row = jnp.zeros((1, model_width), full_type)
-    self_full = (
-        lax.all_gather(self_in.astype(low_type), ("dp", "fsdp"), axis=0, tiled=True),
-        lax.all_gather(self_out.astype(low_type), ("dp", "fsdp"), axis=1, tiled=True),
-        lax.all_gather(self_bias.astype(low_type), ("dp", "fsdp"), axis=1, tiled=True),
-    )
-    self_bias_full = self_full[2].astype(full_type)
+    device_count = lax.axis_size(AXES)
+    own_rows = self_in.shape[0]
+    packed = jnp.concatenate(
+        [
+            self_in,
+            self_out.T,
+            cross_query,
+            cross_key_value,
+            cross_out.T,
+            feed_in,
+            feed_out.T,
+            self_bias.T,
+            cross_bias.T,
+            feed_bias_out[:, None],
+            feed_bias_in.reshape(own_rows, -1),
+        ],
+        axis=1,
+    ).astype(low_type)
+    spare = -packed.shape[1] % 128
+    whole = rows_all(jnp.pad(packed, ((0, 0), (0, spare))))
+    ff = feed_in.shape[1]
+    d = model_width
+    self_full = (whole[:, : 3 * d], whole[:, 3 * d : 4 * d].T)
+    cross_full = (
+        whole[:, 4 * d : 5 * d],
+        whole[:, 5 * d : 7 * d],
+        whole[:, 7 * d : 8 * d].T,
+    )
+    feed_full = (
+        whole[:, 8 * d : 8 * d + ff],
+        whole[:, 8 * d + ff : 8 * d + 2 * ff].T,
+    )
+    at = 8 * d + 2 * ff
+    self_bias_full = whole[:, at : at + 3].T.astype(full_type)
+    cross_bias_full = whole[:, at + 3 : at + 6].T.astype(full_type)
+    feed_bias_out_full = whole[:, at + 6].astype(full_type)
+    feed_bias_in_full = whole[:, at + 7 : at + 7 + ff // d].reshape(ff).astype(full_type)
     projected = (
         jnp.dot(tokens, self_full[0], preferred_element_type=full_type)
         + jnp.concatenate([self_bias_full[0:1], zero_row, self_bias_full[1:2]], axis=1)
@@ -164,13 +241,6 @@
         jnp.dot(self_mixed, self_full[1], preferred_element_type=full_type) + self_bias_full[2]
     )
     first_low = first_sum.astype(low_type)
-    cross_full = (
-        lax.all_gather(cross_query.astype(low_type), ("dp", "fsdp"), axis=0, tiled=True),
-        lax.all_gather(cross_key_value.astype(low_type), ("dp", "fsdp"), axis=0, tiled=True),
-        lax.all_gather(cross_out.astype(low_type), ("dp", "fsdp"), axis=1, tiled=True),
-        lax.all_gather(cross_bias.astype(low_type), ("dp", "fsdp"), axis=1, tiled=True),
-    )
-    cross_bias_full = cross_full[3].astype(full_type)
     cross_queries = (
         jnp.dot(first_low, cross_full[0], preferred_element_type=full_type) + cross_bias_full[0]
     ).astype(low_type)
@@ -190,34 +260,22 @@
         jnp.dot(cross_mixed, cross_full[2], preferred_element_type=full_type) + cross_bias_full[2]
     )
     second_low = second_sum.astype(low_type)
-    feed_full = (
-        lax.all_gather(feed_in.astype(low_type), ("dp", "fsdp"), axis=0, tiled=True),
-        lax.all_gather(feed_out.astype(low_type), ("dp", "fsdp"), axis=1, tiled=True),
-        lax.all_gather(feed_bias_in.astype(low_type), ("dp", "fsdp"), axis=0, tiled=True),
-        lax.all_gather(feed_bias_out.astype(low_type), ("dp", "fsdp"), axis=0, tiled=True),
-    )
-    before = jnp.dot(second_low, feed_full[0], preferred_element_type=full_type) + feed_full[
-        2
-    ].astype(full_type)
+    before = jnp.dot(second_low, feed_full[0], preferred_element_type=full_type) + feed_bias_in_full
     hidden = gelu_tanh(before).astype(low_type)
     output = (
         second_sum
         + branch_scale
         * (
             jnp.dot(hidden, feed_full[1], preferred_element_type=full_type)
-            + feed_full[3].astype(full_type)
-        )
-    ).astype(low_type)
-    feed_back = (
-        lax.all_gather(feed_in.astype(low_type), ("dp", "fsdp"), axis=0, tiled=True),
-        lax.all_gather(feed_out.astype(low_type), ("dp", "fsdp"), axis=1, tiled=True),
-    )
+            + feed_bias_out_full
+        )
+    ).astype(low_type)
     upstream = out_cotangent.astype(full_type)
     feed_signal = (branch_scale * upstream).astype(low_type)
     feed_out_local = jnp.einsum("tf,td->fd", hidden, feed_signal, preferred_element_type=full_type)
     feed_bias_out_local = jnp.sum(feed_signal.astype(full_type), axis=0)
     hidden_grad = jnp.einsum(
-        "td,fd->tf", feed_signal, feed_back[1], preferred_element_type=full_type
+        "td,fd->tf", feed_signal, feed_full[1], preferred_element_type=full_type
     )
     gelu_pull = jax.vjp(gelu_tanh, before)[1]
     before_grad = gelu_pull(hidden_grad)[0].astype(low_type)
@@ -226,25 +284,15 @@
     )
     feed_bias_in_local = jnp.sum(before_grad.astype(full_type), axis=0)
     second_grad = upstream + jnp.einsum(
-        "tf,df->td", before_grad, feed_back[0], preferred_element_type=full_type
-    )
-    feed_owned = (
-        lax.psum_scatter(feed_in_local, ("dp", "fsdp"), scatter_dimension=0, tiled=True),
-        lax.psum_scatter(feed_out_local, ("dp", "fsdp"), scatter_dimension=1, tiled=True),
-        lax.psum_scatter(feed_bias_in_local, ("dp", "fsdp"), scatter_dimension=0, tiled=True),
-        lax.psum_scatter(feed_bias_out_local, ("dp", "fsdp"), scatter_dimension=0, tiled=True),
-    )
-    cross_back = (
-        lax.all_gather(cross_query.astype(low_type), ("dp", "fsdp"), axis=0, tiled=True),
-        lax.all_gather(cross_key_value.astype(low_type), ("dp", "fsdp"), axis=0, tiled=True),
-        lax.all_gather(cross_out.astype(low_type), ("dp", "fsdp"), axis=1, tiled=True),
-    )
+        "tf,df->td", before_grad, feed_full[0], preferred_element_type=full_type
+    )
+    feed_owned = scatter_rows(jnp.concatenate([feed_in_local, feed_out_local.T], axis=1), device_count)
     cross_signal = (branch_scale * second_grad).astype(low_type)
     cross_out_local = jnp.einsum(
         "tc,td->cd", cross_mixed, cross_signal, preferred_element_type=full_type
     )
     cross_mixed_grad = jnp.einsum(
-        "td,cd->tc", cross_signal, cross_back[2], preferred_element_type=full_type
+        "td,cd->tc", cross_signal, cross_full[2], preferred_element_type=full_type
     ).astype(low_type)
     query_part, key_part, value_part = attend_backward(
         cross_queries,
@@ -272,27 +320,21 @@
         ]
     )
     memory_grad = jnp.einsum(
-        "me,ce->mc", memory_signal, cross_back[1], preferred_element_type=full_type
+        "me,ce->mc", memory_signal, cross_full[1], preferred_element_type=full_type
     )
     first_grad = second_grad + jnp.einsum(
-        "td,cd->tc", cross_query_signal, cross_back[0], preferred_element_type=full_type
-    )
-    cross_owned = (
-        lax.psum_scatter(cross_query_local, ("dp", "fsdp"), scatter_dimension=0, tiled=True),
-        lax.psum_scatter(cross_key_value_local, ("dp", "fsdp"), scatter_dimension=0, tiled=True),
-        lax.psum_scatter(cross_out_local, ("dp", "fsdp"), scatter_dimension=1, tiled=True),
-        lax.psum_scatter(cross_bias_local, ("dp", "fsdp"), scatter_dimension=1, tiled=True),
-    )
-    self_back = (
-        lax.all_gather(self_in.astype(low_type), ("dp", "fsdp"), axis=0, tiled=True),
-        lax.all_gather(self_out.astype(low_type), ("dp", "fsdp"), axis=1, tiled=True),
+        "td,cd->tc", cross_query_signal, cross_full[0], preferred_element_type=full_type
+    )
+    cross_owned = scatter_rows(
+        jnp.concatenate([cross_query_local, cross_key_value_local, cross_out_local.T], axis=1),
+        device_count,
     )
     self_signal = (branch_scale * first_grad).astype(low_type)
     self_out_local = jnp.einsum(
         "tc,td->cd", self_mixed, self_signal, preferred_element_type=full_type
     )
     self_mixed_grad = jnp.einsum(
-        "td,cd->tc", self_signal, self_back[1], preferred_element_type=full_type
+        "td,cd->tc", self_signal, self_full[1], preferred_element_type=full_type
     ).astype(low_type)
     query_self, key_self, value_self = attend_backward(
         projected[:, :model_width],
@@ -316,28 +358,37 @@
         ]
     )
     tokens_grad = first_grad + jnp.einsum(
-        "te,ce->tc", projected_signal, self_back[0], preferred_element_type=full_type
-    )
-    self_owned = (
-        lax.psum_scatter(self_in_local, ("dp", "fsdp"), scatter_dimension=0, tiled=True),
-        lax.psum_scatter(self_out_local, ("dp", "fsdp"), scatter_dimension=1, tiled=True),
-        lax.psum_scatter(self_bias_local, ("dp", "fsdp"), scatter_dimension=1, tiled=True),
-    )
+        "te,ce->tc", projected_signal, self_full[0], preferred_element_type=full_type
+    )
+    bias_columns = jnp.concatenate(
+        [
+            self_bias_local.T,
+            cross_bias_local.T,
+            feed_bias_out_local[:, None],
+            feed_bias_in_local.reshape(d, -1),
+        ],
+        axis=1,
+    )
+    bias_columns = jnp.pad(bias_columns, ((0, 0), (0, -bias_columns.shape[1] % 128)))
+    self_owned = scatter_rows(
+        jnp.concatenate([self_in_local, self_out_local.T, bias_columns], axis=1), device_count
+    )
+    bias_owned = self_owned[:, 4 * d :]
     return (
         output,
         tokens_grad,
         memory_grad,
-        self_owned[0],
-        self_owned[1],
-        self_owned[2],
-        cross_owned[0],
-        cross_owned[1],
-        cross_owned[2],
-        cross_owned[3],
-        feed_owned[0],
-        feed_owned[1],
-        feed_owned[2],
-        feed_owned[3],
+        self_owned[:, : 3 * d],
+        self_owned[:, 3 * d : 4 * d].T,
+        bias_owned[:, 0:3].T,
+        cross_owned[:, :d],
+        cross_owned[:, d : 3 * d],
+        cross_owned[:, 3 * d :].T,
+        bias_owned[:, 3:6].T,
+        feed_owned[:, :ff],
+        feed_owned[:, ff:].T,
+        bias_owned[:, 7 : 7 + ff // d].reshape(feed_bias_in.shape),
+        bias_owned[:, 6],
     )
 
 

time: 1930 us -> 705 us (0.37)
  waiting for transfers between devices: 1090 us -> 110 us
  blocking collectives: 286 us -> 0 us
  starting transfers between devices: 0.79 us -> 27.7 us
  matrix products: 385 us -> 405 us
    reduce_scatter x5 -> x0, waiting for transfers between devices: 684 us -> none  [the longest x1 142 us: on_device(): lax.psum_scatter(feed_out_local, ('dp', 'fsdp'), scatter_dimension=1, til...]
    unnamed x17 -> x1, waiting for transfers between devices: 408 us -> 0.02 us
    all_gather x5 -> x0, blocking collectives: 205 us -> none  [the longest x1 43.7 us: on_device(): lax.all_gather(cross_out.astype(low_type), ('dp', 'fsdp'), axis=1, tiled=...]
    unnamed x2 -> x0, blocking collectives: 80.6 us -> none
    all_gather x4 -> x1, waiting for transfers between devices: 0.03 us -> 73.4 us  [rows_all(): return lax.all_gather(shard, AXES, axis=0, tiled=True)]
    ppermute x0 -> x30, waiting for transfers between devices: none -> 36.8 us  [sum_to_owners(): lax.ppermute(away.astype(jnp.bfloat16), AXES, pairs)]
    ppermute x0 -> x30, starting transfers between devices: none -> 27.7 us  [sum_to_owners(): lax.ppermute(away.astype(jnp.bfloat16), AXES, pairs)]
  transfers between devices with their start and end apart: 13 -> 31, of which waited for: 9 -> 19; matrix products, arithmetic and copies ran while one was open for 10% -> 34% of each run, Pallas kernels for 0% -> 0%
where the time goes in v1:
time: 705 us; the launch traced here: 700 us
  matrix products  405 us (57%)
  waiting for transfers between devices  110 us (16%)
  local copies, waits for them, and re-layouts  79.4 us (11%)
  other arithmetic  60.1 us (9%)
  starting transfers between devices  27.7 us (4%)
  between operations  16.6 us (2%)
    dot_general x4, matrix products, per_block(): jnp.einsum('hqk,qhd->khd', score_grad, query_block, preferred_element_typ...  94.8 us
    dot_general x4, matrix products, per_block(): jnp.einsum('hqk,khd->qhd', score_grad, key_heads, preferred_element_type=...  90.7 us
    all_gather x1, waiting for transfers between devices, rows_all(): return lax.all_gather(shard, AXES, axis=0, tiled=True)  73.4 us
    dot_general x8, matrix products, block_scores(): jnp.einsum('qhd,khd->hqk', query_block, key_heads, preferred_element_type...  54.5 us
    ppermute x30, waiting for transfers between devices, sum_to_owners(): lax.ppermute(away.astype(jnp.bfloat16), AXES, pairs)  36.8 us
    dot_general x4, matrix products, per_block(): jnp.einsum('hqk,qhd->khd', chances.astype(jnp.bfloat16), incoming_block,...  36 us
    dot_general x4, matrix products, per_block(): jnp.einsum('qhd,khd->hqk', incoming_block, value_heads, preferred_element...  32.5 us
    ppermute x30, starting transfers between devices, sum_to_owners(): lax.ppermute(away.astype(jnp.bfloat16), AXES, pairs)  27.7 us
  transfers between devices with their start and end apart: 31, of which 19 were waited for; matrix products, arithmetic and copies ran while one was open for 34% of the time, Pallas kernels for 0%

profile of v1, /device:TPU:0, one launch (start us, length us, event | category | flops | bytes accessed | tf_op | source)
XLA Modules:
  0.0 699.9 jit_solution(10869884769093069903)
XLA Ops:
  24.0 73.4 %all-gather.2.cloned.1.call-done = bf16[512,8320]{1,0:T(8,128)(2,1)} async-done(((bf16[16,8320]{1,0:T(8,128)(2,1)}), bf16[512,8320]{1,0:T(8,128)(2,1)}) %all-gather.2.cloned.1.call-update) | async-done | bytes 8519696 | tf_op jit(solution)/shard_map/all_gather | solution.py:11
  111.8 32.0 %while.54 = (s32[]{:T(128)}, bf16[2,512,8,64]{1,3,2,0:T(8,128)(2,1)}, f32[2,8,512]{2,1,0:T(8,128)S(1)}, s32[2,512]{1,0:T(2,128)S(1)}, s32[1024]{0:T(1024)S(1)}, ...) while((s32[]{:T(128)}, ...), condition=%wide.region_5.6_spmd, body=%wide.region_2.5_spmd.sunk | while | flops 1125904896 | bytes 55721084 | solution.py:109
  122.0 5.8 fusion.262
  138.0 5.8 fusion.262
  163.6 29.1 %while.55 = (s32[]{:T(128)}, bf16[2,512,8,64]{1,3,2,0:T(8,128)(2,1)}, f32[2,8,512]{2,1,0:T(8,128)S(1)}, s32[2,512]{1,0:T(2,128)S(1)}, s32[1024]{0:T(1024)S(1)}, ...) while((s32[]{:T(128)}, ...), condition=%wide.region_11.12_spmd, body=%wide.region_8.11_spmd.sunk | while | flops 1124855808 | bytes 55716964 | solution.py:109
  172.3 5.8 fusion.267
  186.9 5.8 fusion.267
  201.0 8.3 %multiply_convert_fusion.2 = (bf16[1024,2048]{1,0:T(8,128)(2,1)}, f32[1024,2048]{1,0:T(8,128)S(1)}) fusion(f32[2048]{0:T(1024)S(1)} %reshape.439, bf16[512,8320]{1,0:T(8,128)(2,1)} %all-gather.2.cloned.1.call-done, f32[1024,512]{1,0:T(8,128)S(1)} %multiply_add_fusion), kind=kOutput, calls=%fused_computation.120 | convolution fusion | flops 2168979456 | bytes 16785408 | tf_op jit(solution)/shard_map/dot_general | solution.py:263
  209.4 7.9 %convert_reduce_fusion = (f32[2048]{0:T(1024)}, bf16[1024,2048]{1,0:T(8,128)(2,1)S(1)}) fusion(f32[1024,2048]{1,0:T(8,128)S(1)} %get-tuple-element.802, f32[2048]{0:T(1024)S(1)} %reshape.439, bf16[512,8320]{1,0:T(8,128)(2,1)S(1)} %bitcast.440, bf16[1024,512]{1,0:T(8,128)(2,1)S(1)} %copy-done.24, f32[1024]{0:T(1024)S(1)} %copy-done.44), kind=kOutput, calls=%fused_computation.119 | convolution fusion | flops 2197288960 | bytes 15749120 | tf_op jit(solution)/shard_map/td,fd->tf/dot_general | solution.py:277
  234.2 147.5 %while.56 = (s32[]{:T(128)}, f32[1024,8,64]{0,2,1:T(8,128)}, f32[1024,8,64]{0,2,1:T(8,128)}, bf16[2,512,8,64]{1,3,2,0:T(8,128)(2,1)}, bf16[2,512,8,64]{1,3,2,0:T...) while((s32[]{:T(128)}, f32[1024,8,64]{0,2,1:T(8,128)}, ...), condition=%wide.region_14.15_spmd.clone, body=%wide.region_12.14_spmd.clone.sunk | while | flops 2745706496 | bytes 200339088 | solution.py:150
  235.0 9.5 %subtract_exponential_fusion.6 = f32[8,512,1024]{2,1,0:T(8,128)} fusion(bf16[1024,8,64]{0,2,1:T(8,128)(2,1)} %get-tuple-element.1151, f32[8,512]{1,0:T(8,128)S(1)} %dynamic-slice_bitcast_fusion.4, pred[512,1024]{1,0:T(8,128)(4,1)S(1)} %broadcast_compare_fusion.5, bf16[2,512,8,64]{1,3,2,0:T(8,128)(2,1)} %get-tuple-element.1148, s32[]{:T(128)} %get-tuple-element.1131), kind=kOutput, calls=%fused_computation.42.clone.1 | convolution fusion | flops 549453824 | bytes 18891264 | tf_op jit(solution)/shard_map/while/body/eval_jaxpr/qhd,khd->hqk/dot_general | solution.py:84
  244.6 8.1 %fusion.278 = f32[8,512,1024]{2,1,0:T(8,128)} fusion(bf16[1024,8,64]{0,2,1:T(8,128)(2,1)S(1)} %get-tuple-element.1154, bf16[2,512,8,64]{1,3,2,0:T(8,128)(2,1)S(1)} %get-tuple-element.1153, s32[]{:T(128)} %get-tuple-element.1131), kind=kOutput, calls=%fused_computation.55.clone.1 | convolution fusion | flops 536870912 | bytes 18350084 | tf_op jit(solution)/shard_map/while/body/eval_jaxpr/qhd,khd->hqk/dot_general | solution.py:127
  252.7 23.4 %bitcast_add_fusion.38 = f32[1024,8,64]{0,2,1:T(8,128)} fusion(f32[1024,8,64]{0,2,1:T(8,128)} %get-tuple-element.1132, f32[8,512,1024]{2,1,0:T(8,128)} %subtract_exponential_fusion.6, f32[8,512,1024]{2,1,0:T(8,128)} %fusion.278, pred[]{:T(512)S(6)} %compare.16, bf16[2,512,8,64]{1,3,2,0:T(8,128)(2,1)} %get-tuple-element.1148, s32[]{:T(128)} %get-tuple-element.1131), kind=kOutput, calls=%fused_computation.50.clone.1 | convolution fusion | flops 558896128 | bytes 71827968 | tf_op jit(solution)/shard_map/while/body/eval_jaxpr/hqk,qhd->khd/dot_general | solution.py:135
  276.1 22.7 %fusion.279 = bf16[2,512,8,64]{1,3,2,0:T(8,128)(2,1)} fusion(bf16[2,512,8,64]{1,3,2,0:T(8,128)(2,1)} %get-tuple-element.1134, s32[]{:T(128)} %get-tuple-element.1131, bf16[1024,8,64]{0,2,1:T(8,128)(2,1)} %get-tuple-element.1151, f32[8,512,1024]{2,1,0:T(8,128)} %subtract_exponential_fusion.6, f32[8,512,1024]{2,1,0:T(8,128)} %fusion.278), kind=kOutput, calls=%fused_computation.52.clone.1 | convolution fusion | flops 557847552 | bytes 69206528 | tf_op jit(solution)/shard_map/while/body/eval_jaxpr/hqk,khd->qhd/dot_general | solution.py:132
  298.8 8.7 %bitcast_add_fusion.39 = f32[1024,8,64]{0,2,1:T(8,128)} fusion(f32[1024,8,64]{0,2,1:T(8,128)} %get-tuple-element.1133, f32[8,512,1024]{2,1,0:T(8,128)} %subtract_exponential_fusion.6, pred[]{:T(512)S(6)} %compare.16, bf16[2,512,8,64]{1,3,2,0:T(8,128)(2,1)S(1)} %get-tuple-element.1153, s32[]{:T(128)} %get-tuple-element.1131), kind=kOutput, calls=%fused_computation.49.clone.1 | convolution fusion | flops 542113792 | bytes 21495812 | tf_op jit(solution)/shard_map/while/body/eval_jaxpr/hqk,qhd->khd/dot_general | solution.py:138
  307.9 9.5 %subtract_exponential_fusion.6 = f32[8,512,1024]{2,1,0:T(8,128)} fusion(bf16[1024,8,64]{0,2,1:T(8,128)(2,1)} %get-tuple-element.1151, f32[8,512]{1,0:T(8,128)S(1)} %dynamic-slice_bitcast_fusion.4, pred[512,1024]{1,0:T(8,128)(4,1)S(1)} %broadcast_compare_fusion.5, bf16[2,512,8,64]{1,3,2,0:T(8,128)(2,1)} %get-tuple-element.1148, s32[]{:T(128)} %get-tuple-element.1131), kind=kOutput, calls=%fused_computation.42.clone.1 | convolution fusion | flops 549453824 | bytes 18891264 | tf_op jit(solution)/shard_map/while/body/eval_jaxpr/qhd,khd->hqk/dot_general | solution.py:84
  317.4 8.1 %fusion.278 = f32[8,512,1024]{2,1,0:T(8,128)} fusion(bf16[1024,8,64]{0,2,1:T(8,128)(2,1)S(1)} %get-tuple-element.1154, bf16[2,512,8,64]{1,3,2,0:T(8,128)(2,1)S(1)} %get-tuple-element.1153, s32[]{:T(128)} %get-tuple-element.1131), kind=kOutput, calls=%fused_computation.55.clone.1 | convolution fusion | flops 536870912 | bytes 18350084 | tf_op jit(solution)/shard_map/while/body/eval_jaxpr/qhd,khd->hqk/dot_general | solution.py:127
  325.6 24.1 %bitcast_add_fusion.38 = f32[1024,8,64]{0,2,1:T(8,128)} fusion(f32[1024,8,64]{0,2,1:T(8,128)} %get-tuple-element.1132, f32[8,512,1024]{2,1,0:T(8,128)} %subtract_exponential_fusion.6, f32[8,512,1024]{2,1,0:T(8,128)} %fusion.278, pred[]{:T(512)S(6)} %compare.16, bf16[2,512,8,64]{1,3,2,0:T(8,128)(2,1)} %get-tuple-element.1148, s32[]{:T(128)} %get-tuple-element.1131), kind=kOutput, calls=%fused_computation.50.clone.1 | convolution fusion | flops 558896128 | bytes 71827968 | tf_op jit(solution)/shard_map/while/body/eval_jaxpr/hqk,qhd->khd/dot_general | solution.py:135
  349.6 22.7 %fusion.279 = bf16[2,512,8,64]{1,3,2,0:T(8,128)(2,1)} fusion(bf16[2,512,8,64]{1,3,2,0:T(8,128)(2,1)} %get-tuple-element.1134, s32[]{:T(128)} %get-tuple-element.1131, bf16[1024,8,64]{0,2,1:T(8,128)(2,1)} %get-tuple-element.1151, f32[8,512,1024]{2,1,0:T(8,128)} %subtract_exponential_fusion.6, f32[8,512,1024]{2,1,0:T(8,128)} %fusion.278), kind=kOutput, calls=%fused_computation.52.clone.1 | convolution fusion | flops 557847552 | bytes 69206528 | tf_op jit(solution)/shard_map/while/body/eval_jaxpr/hqk,khd->qhd/dot_general | solution.py:132
  372.3 9.3 %bitcast_add_fusion.39 = f32[1024,8,64]{0,2,1:T(8,128)} fusion(f32[1024,8,64]{0,2,1:T(8,128)} %get-tuple-element.1133, f32[8,512,1024]{2,1,0:T(8,128)} %subtract_exponential_fusion.6, pred[]{:T(512)S(6)} %compare.16, bf16[2,512,8,64]{1,3,2,0:T(8,128)(2,1)S(1)} %get-tuple-element.1153, s32[]{:T(128)} %get-tuple-element.1131), kind=kOutput, calls=%fused_computation.49.clone.1 | convolution fusion | flops 542113792 | bytes 21495812 | tf_op jit(solution)/shard_map/while/body/eval_jaxpr/hqk,qhd->khd/dot_general | solution.py:138
  427.8 150.1 %while.57 = (s32[]{:T(128)}, f32[1024,8,64]{0,2,1:T(8,128)}, f32[1024,8,64]{0,2,1:T(8,128)}, bf16[2,512,8,64]{1,3,2,0:T(8,128)(2,1)}, bf16[2,512,8,64]{1,3,2,0:T...) while((s32[]{:T(128)}, f32[1024,8,64]{0,2,1:T(8,128)}, ...), condition=%wide.region_17.18_spmd.clone, body=%wide.region_15.17_spmd.clone.sunk | while | flops 2746755584 | bytes 200343216 | solution.py:150
  429.9 9.5 %subtract_exponential_fusion.7 = f32[8,512,1024]{2,1,0:T(8,128)} fusion(bf16[1024,8,64]{0,2,1:T(8,128)(2,1)} %get-tuple-element.1193, f32[8,512]{1,0:T(8,128)S(1)} %dynamic-slice_bitcast_fusion.5, pred[512,1024]{1,0:T(8,128)(4,1)S(1)} %fusion.290, bf16[2,512,8,64]{1,3,2,0:T(8,128)(2,1)} %get-tuple-element.1189, s32[]{:T(128)} %get-tuple-element.1171), kind=kOutput, calls=%fused_computation.77.clone.1 | convolution fusion | flops 549453824 | bytes 18891264 | tf_op jit(solution)/shard_map/while/body/eval_jaxpr/qhd,khd->hqk/dot_general | solution.py:84
  439.4 8.1 %fusion.291 = f32[8,512,1024]{2,1,0:T(8,128)} fusion(bf16[1024,8,64]{0,2,1:T(8,128)(2,1)S(1)} %get-tuple-element.1196, bf16[2,512,8,64]{1,3,2,0:T(8,128)(2,1)S(1)} %get-tuple-element.1195, s32[]{:T(128)} %get-tuple-element.1171), kind=kOutput, calls=%fused_computation.91.clone.1 | convolution fusion | flops 536870912 | bytes 18350084 | tf_op jit(solution)/shard_map/while/body/eval_jaxpr/qhd,khd->hqk/dot_general | solution.py:127
  447.5 23.4 %bitcast_add_fusion.40 = f32[1024,8,64]{0,2,1:T(8,128)} fusion(f32[1024,8,64]{0,2,1:T(8,128)} %get-tuple-element.1172, f32[8,512,1024]{2,1,0:T(8,128)} %subtract_exponential_fusion.7, f32[8,512,1024]{2,1,0:T(8,128)} %fusion.291, pred[]{:T(512)S(6)} %compare.17, bf16[2,512,8,64]{1,3,2,0:T(8,128)(2,1)} %get-tuple-element.1189, s32[]{:T(128)} %get-tuple-element.1171), kind=kOutput, calls=%fused_computation.85.clone.1 | convolution fusion | flops 558896128 | bytes 71827968 | tf_op jit(solution)/shard_map/while/body/eval_jaxpr/hqk,qhd->khd/dot_general | solution.py:135
  470.9 22.7 %fusion.292 = bf16[2,512,8,64]{1,3,2,0:T(8,128)(2,1)} fusion(bf16[2,512,8,64]{1,3,2,0:T(8,128)(2,1)} %get-tuple-element.1174, s32[]{:T(128)} %get-tuple-element.1171, bf16[1024,8,64]{0,2,1:T(8,128)(2,1)} %get-tuple-element.1193, f32[8,512,1024]{2,1,0:T(8,128)} %subtract_exponential_fusion.7, f32[8,512,1024]{2,1,0:T(8,128)} %fusion.291), kind=kOutput, calls=%fused_computation.89.clone.1 | convolution fusion | flops 557847552 | bytes 69206528 | tf_op jit(solution)/shard_map/while/body/eval_jaxpr/hqk,khd->qhd/dot_general | solution.py:132
  493.5 8.7 %bitcast_add_fusion.41 = f32[1024,8,64]{0,2,1:T(8,128)} fusion(f32[1024,8,64]{0,2,1:T(8,128)} %get-tuple-element.1173, f32[8,512,1024]{2,1,0:T(8,128)} %subtract_exponential_fusion.7, pred[]{:T(512)S(6)} %compare.17, bf16[2,512,8,64]{1,3,2,0:T(8,128)(2,1)S(1)} %get-tuple-element.1195, s32[]{:T(128)} %get-tuple-element.1171), kind=kOutput, calls=%fused_computation.84.clone.1 | convolution fusion | flops 542113792 | bytes 21495812 | tf_op jit(solution)/shard_map/while/body/eval_jaxpr/hqk,qhd->khd/dot_general | solution.py:138
  504.1 9.5 %subtract_exponential_fusion.7 = f32[8,512,1024]{2,1,0:T(8,128)} fusion(bf16[1024,8,64]{0,2,1:T(8,128)(2,1)} %get-tuple-element.1193, f32[8,512]{1,0:T(8,128)S(1)} %dynamic-slice_bitcast_fusion.5, pred[512,1024]{1,0:T(8,128)(4,1)S(1)} %fusion.290, bf16[2,512,8,64]{1,3,2,0:T(8,128)(2,1)} %get-tuple-element.1189, s32[]{:T(128)} %get-tuple-element.1171), kind=kOutput, calls=%fused_computation.77.clone.1 | convolution fusion | flops 549453824 | bytes 18891264 | tf_op jit(solution)/shard_map/while/body/eval_jaxpr/qhd,khd->hqk/dot_general | solution.py:84
  513.6 8.1 %fusion.291 = f32[8,512,1024]{2,1,0:T(8,128)} fusion(bf16[1024,8,64]{0,2,1:T(8,128)(2,1)S(1)} %get-tuple-element.1196, bf16[2,512,8,64]{1,3,2,0:T(8,128)(2,1)S(1)} %get-tuple-element.1195, s32[]{:T(128)} %get-tuple-element.1171), kind=kOutput, calls=%fused_computation.91.clone.1 | convolution fusion | flops 536870912 | bytes 18350084 | tf_op jit(solution)/shard_map/while/body/eval_jaxpr/qhd,khd->hqk/dot_general | solution.py:127
  521.8 24.0 %bitcast_add_fusion.40 = f32[1024,8,64]{0,2,1:T(8,128)} fusion(f32[1024,8,64]{0,2,1:T(8,128)} %get-tuple-element.1172, f32[8,512,1024]{2,1,0:T(8,128)} %subtract_exponential_fusion.7, f32[8,512,1024]{2,1,0:T(8,128)} %fusion.291, pred[]{:T(512)S(6)} %compare.17, bf16[2,512,8,64]{1,3,2,0:T(8,128)(2,1)} %get-tuple-element.1189, s32[]{:T(128)} %get-tuple-element.1171), kind=kOutput, calls=%fused_computation.85.clone.1 | convolution fusion | flops 558896128 | bytes 71827968 | tf_op jit(solution)/shard_map/while/body/eval_jaxpr/hqk,qhd->khd/dot_general | solution.py:135
  545.7 22.7 %fusion.292 = bf16[2,512,8,64]{1,3,2,0:T(8,128)(2,1)} fusion(bf16[2,512,8,64]{1,3,2,0:T(8,128)(2,1)} %get-tuple-element.1174, s32[]{:T(128)} %get-tuple-element.1171, bf16[1024,8,64]{0,2,1:T(8,128)(2,1)} %get-tuple-element.1193, f32[8,512,1024]{2,1,0:T(8,128)} %subtract_exponential_fusion.7, f32[8,512,1024]{2,1,0:T(8,128)} %fusion.291), kind=kOutput, calls=%fused_computation.89.clone.1 | convolution fusion | flops 557847552 | bytes 69206528 | tf_op jit(solution)/shard_map/while/body/eval_jaxpr/hqk,khd->qhd/dot_general | solution.py:132
  568.4 9.3 %bitcast_add_fusion.41 = f32[1024,8,64]{0,2,1:T(8,128)} fusion(f32[1024,8,64]{0,2,1:T(8,128)} %get-tuple-element.1173, f32[8,512,1024]{2,1,0:T(8,128)} %subtract_exponential_fusion.7, pred[]{:T(512)S(6)} %compare.17, bf16[2,512,8,64]{1,3,2,0:T(8,128)(2,1)S(1)} %get-tuple-element.1195, s32[]{:T(128)} %get-tuple-element.1171), kind=kOutput, calls=%fused_computation.84.clone.1 | convolution fusion | flops 542113792 | bytes 21495812 | tf_op jit(solution)/shard_map/while/body/eval_jaxpr/hqk,qhd->khd/dot_general | solution.py:138
  602.5 5.1 add_convert_fusion.2
  (409 shorter events, 272.0 us)
Async XLA Ops:
  7.2 152.5 %copy-start = (bf16[1024,512]{1,0:T(8,128)(2,1)S(1)}, bf16[1024,512]{1,0:T(8,128)(2,1)}, u32[]{:S(2)}) copy-start(bf16[1024,512]{1,0:T(8,128)(2,1)} %param.26) | copy-start | bytes 3145732
  7.2 90.2 %all-gather.2.cloned.1.call-start = ((), (), s32[]{:S(2)}) async-start(), calls=%async_computation | async-start | bytes 8785920 | tf_op jit(solution)/shard_map/all_gather | solution.py:11
  392.3 262.2 %collective-permute-start.25 = (bf16[2,2,2,2,16,2048]{5,4,3,2,0,1:T(8,128)(2,1)}, bf16[2,2,2,2,16,2048]{5,4,3,2,0,1:T(8,128)(2,1)}, u32[]{:S(2)}, u32[]{:S(2)}) collective-permute-start(bf16[2,2,2,2,16,2048]{5,4,3,2,0,1:T(8,128)(2,1)} %fusion.132), channel_id=1, source_target_pairs={{0,1},{1,0},{2,3},{3,2},{4,5},{5,4},{6,7},{7,6},{8,9},{9,8},{10,11... | collective-permute-start | bytes 3145736 | tf_op jit(solution)/shard_map/ppermute | solution.py:30
  397.0 260.7 %collective-permute-start.20 = (bf16[2,2,2,2,16,2048]{5,4,3,2,1,0:T(8,128)(2,1)}, bf16[2,2,2,2,16,2048]{5,4,3,2,1,0:T(8,128)(2,1)}, u32[]{:S(2)}, u32[]{:S(2)}) collective-permute-start(bf16[2,2,2,2,16,2048]{5,4,3,2,1,0:T(8,128)(2,1)} %fusion.133), channel_id=1, source_target_pairs={{0,1},{1,0},{2,3},{3,2},{4,5},{5,4},{6,7},{7,6},{8,9},{9,8},{10,11... | collective-permute-start | bytes 3145736 | tf_op jit(solution)/shard_map/ppermute | solution.py:30
  408.3 199.5 %collective-permute-start.15 = (bf16[2,2,2,2,16,1024]{5,4,3,2,0,1:T(8,128)(2,1)}, bf16[2,2,2,2,16,1024]{5,4,3,2,0,1:T(8,128)(2,1)}, u32[]{:S(2)}, u32[]{:S(2)}) collective-permute-start(bf16[2,2,2,2,16,1024]{5,4,3,2,0,1:T(8,128)(2,1)} %fusion.140), channel_id=1, source_target_pairs={{0,1},{1,0},{2,3},{3,2},{4,5},{5,4},{6,7},{7,6},{8,9},{9,8},{10,11... | collective-permute-start | bytes 1572872 | tf_op jit(solution)/shard_map/ppermute | solution.py:30
  413.7 196.6 %collective-permute-start.10 = (bf16[2,2,2,2,16,1024]{5,4,3,2,1,0:T(8,128)(2,1)}, bf16[2,2,2,2,16,1024]{5,4,3,2,1,0:T(8,128)(2,1)}, u32[]{:S(2)}, u32[]{:S(2)}) collective-permute-start(bf16[2,2,2,2,16,1024]{5,4,3,2,1,0:T(8,128)(2,1)} %fusion.137), channel_id=1, source_target_pairs={{0,1},{1,0},{2,3},{3,2},{4,5},{5,4},{6,7},{7,6},{8,9},{9,8},{10,11... | collective-permute-start | bytes 1572872 | tf_op jit(solution)/shard_map/ppermute | solution.py:30
  587.3 25.7 %collective-permute-start = (bf16[2,2,2,2,16,1024]{5,4,3,2,1,0:T(8,128)(2,1)}, bf16[2,2,2,2,16,1024]{5,4,3,2,1,0:T(8,128)(2,1)}, u32[]{:S(2)}, u32[]{:S(2)}) collective-permute-start(bf16[2,2,2,2,16,1024]{5,4,3,2,1,0:T(8,128)(2,1)} %fusion.141), channel_id=1, source_target_pairs={{0,1},{1,0},{2,3},{3,2},{4,5},{5,4},{6,7},{7,6},{8,9},{9,8},{10,11... | collective-permute-start | bytes 1572872 | tf_op jit(solution)/shard_map/ppermute | solution.py:30
  607.8 7.3 %collective-permute-start.5 = (bf16[2,2,2,2,16,1152]{5,4,3,2,1,0:T(8,128)(2,1)S(1)}, bf16[2,2,2,2,16,1152]{5,4,3,2,1,0:T(8,128)(2,1)S(1)}, u32[]{:S(2)}, u32[]{:S(2)}) collective-permute-start(bf16[2,2,2,2,16,1152]{5,4,3,2,1,0:T(8,128)(2,1)S(1)} %fusion.136), channel_id=1, source_target_pairs={{0,1},{1,0},{2,3},{3,2},{4,5},{5,4},{6,7},{7,6},{8,9},{9,8},{10,11... | collective-permute-start | bytes 1769480 | tf_op jit(solution)/shard_map/ppermute | solution.py:30
  610.4 8.5 %collective-permute-start.16 = (bf16[2,2,2,16,1024]{4,3,2,1,0:T(8,128)(2,1)S(1)}, bf16[2,2,2,16,1024]{4,3,2,1,0:T(8,128)(2,1)S(1)}, u32[]{:S(2)}, u32[]{:S(2)}) collective-permute-start(bf16[2,2,2,16,1024]{4,3,2,1,0:T(8,128)(2,1)S(1)} %fusion.157), channel_id=1, source_target_pairs={{0,8},{1,9},{2,10},{3,11},{4,12},{5,13},{6,14},{7,15},{8,0},{9,1},... | collective-permute-start | bytes 786440 | tf_op jit(solution)/shard_map/ppermute | solution.py:30
  613.0 9.2 %collective-permute-start.11 = (bf16[2,2,2,16,1024]{4,3,2,1,0:T(8,128)(2,1)S(1)}, bf16[2,2,2,16,1024]{4,3,2,1,0:T(8,128)(2,1)S(1)}, u32[]{:S(2)}, u32[]{:S(2)}) collective-permute-start(bf16[2,2,2,16,1024]{4,3,2,1,0:T(8,128)(2,1)S(1)} %fusion.156), channel_id=1, source_target_pairs={{0,16},{1,17},{2,18},{3,19},{4,20},{5,21},{6,22},{7,23},{8,24},{9,... | collective-permute-start | bytes 786440 | tf_op jit(solution)/shard_map/ppermute | solution.py:30
  615.1 12.7 %collective-permute-start.1 = (bf16[2,2,2,16,1024]{4,3,2,1,0:T(8,128)(2,1)S(1)}, bf16[2,2,2,16,1024]{4,3,2,1,0:T(8,128)(2,1)S(1)}, u32[]{:S(2)}, u32[]{:S(2)}) collective-permute-start(bf16[2,2,2,16,1024]{4,3,2,1,0:T(8,128)(2,1)S(1)} %fusion.155), channel_id=1, source_target_pairs={{0,16},{1,17},{2,18},{3,19},{4,20},{5,21},{6,22},{7,23},{8,24},{9,... | collective-permute-start | bytes 786440 | tf_op jit(solution)/shard_map/ppermute | solution.py:30
  618.9 9.8 %collective-permute-start.6 = (bf16[2,2,2,16,1152]{4,3,2,1,0:T(8,128)(2,1)S(1)}, bf16[2,2,2,16,1152]{4,3,2,1,0:T(8,128)(2,1)S(1)}, u32[]{:S(2)}, u32[]{:S(2)}) collective-permute-start(bf16[2,2,2,16,1152]{4,3,2,1,0:T(8,128)(2,1)S(1)} %fusion.154), channel_id=1, source_target_pairs={{0,8},{1,9},{2,10},{3,11},{4,12},{5,13},{6,14},{7,15},{8,0},{9,1},... | collective-permute-start | bytes 884744 | tf_op jit(solution)/shard_map/ppermute | solution.py:30
  622.2 8.2 %collective-permute-start.17 = (bf16[2,2,16,1024]{3,2,1,0:T(8,128)(2,1)S(1)}, bf16[2,2,16,1024]{3,2,1,0:T(8,128)(2,1)S(1)}, u32[]{:S(2)}, u32[]{:S(2)}) collective-permute-start(bf16[2,2,16,1024]{3,2,1,0:T(8,128)(2,1)S(1)} %fusion.163), channel_id=1, source_target_pairs={{0,16},{1,17},{2,18},{3,19},{4,20},{5,21},{6,22},{7,23},{8,24},{9,... | collective-permute-start | bytes 393224 | tf_op jit(solution)/shard_map/ppermute | solution.py:30
  627.8 5.0 collective-permute-start.12
  628.7 6.1 collective-permute-start.2
  630.4 22.5 %collective-permute-start.7 = (bf16[2,2,16,1152]{3,2,1,0:T(8,128)(2,1)S(1)}, bf16[2,2,16,1152]{3,2,1,0:T(8,128)(2,1)S(1)}, u32[]{:S(2)}, u32[]{:S(2)}) collective-permute-start(bf16[2,2,16,1152]{3,2,1,0:T(8,128)(2,1)S(1)} %fusion.160), channel_id=1, source_target_pairs={{0,16},{1,17},{2,18},{3,19},{4,20},{5,21},{6,22},{7,23},{8,24},{9,... | collective-permute-start | bytes 442376 | tf_op jit(solution)/shard_map/ppermute | solution.py:30
  632.8 7.9 %collective-permute-start.18 = (bf16[2,16,1024]{2,1,0:T(8,128)(2,1)S(1)}, bf16[2,16,1024]{2,1,0:T(8,128)(2,1)S(1)}, u32[]{:S(2)}, u32[]{:S(2)}) collective-permute-start(bf16[2,16,1024]{2,1,0:T(8,128)(2,1)S(1)} %fusion.170), channel_id=1, source_target_pairs={{0,4},{1,5},{2,6},{3,7},{4,0},{5,1},{6,2},{7,3},{8,12},{9,13},{10,... | collective-permute-start | bytes 196616 | tf_op jit(solution)/shard_map/ppermute | solution.py:30
  634.8 6.7 collective-permute-start.13
  640.7 5.3 collective-permute-start.3
  641.5 4.6 collective-permute-start.19
  646.0 4.7 collective-permute-start.14
  646.1 5.0 collective-permute-start.4
  653.0 6.2 collective-permute-start.8
  657.1 10.2 %collective-permute-start.26 = (bf16[2,2,2,16,2048]{4,3,2,1,0:T(8,128)(2,1)}, bf16[2,2,2,16,2048]{4,3,2,1,0:T(8,128)(2,1)}, u32[]{:S(2)}, u32[]{:S(2)}) collective-permute-start(bf16[2,2,2,16,2048]{4,3,2,1,0:T(8,128)(2,1)} %fusion.139), channel_id=1, source_target_pairs={{0,8},{1,9},{2,10},{3,11},{4,12},{5,13},{6,14},{7,15},{8,0},{9,1},... | collective-permute-start | bytes 1572872 | tf_op jit(solution)/shard_map/ppermute | solution.py:30
  659.2 4.0 collective-permute-start.9
  660.6 11.6 %collective-permute-start.21 = (bf16[2,2,2,16,2048]{4,3,2,1,0:T(8,128)(2,1)}, bf16[2,2,2,16,2048]{4,3,2,1,0:T(8,128)(2,1)}, u32[]{:S(2)}, u32[]{:S(2)}) collective-permute-start(bf16[2,2,2,16,2048]{4,3,2,1,0:T(8,128)(2,1)} %fusion.138), channel_id=1, source_target_pairs={{0,16},{1,17},{2,18},{3,19},{4,20},{5,21},{6,22},{7,23},{8,24},{9,... | collective-permute-start | bytes 1572872 | tf_op jit(solution)/shard_map/ppermute | solution.py:30
  668.8 6.4 collective-permute-start.27
  673.5 6.4 collective-permute-start.22
  675.3 7.3 %collective-permute-start.28 = (bf16[2,16,2048]{2,1,0:T(8,128)(2,1)S(1)}, bf16[2,16,2048]{2,1,0:T(8,128)(2,1)S(1)}, u32[]{:S(2)}, u32[]{:S(2)}) collective-permute-start(bf16[2,16,2048]{2,1,0:T(8,128)(2,1)S(1)} %fusion.165), channel_id=1, source_target_pairs={{0,4},{1,5},{2,6},{3,7},{4,0},{5,1},{6,2},{7,3},{8,12},{9,13},{10,... | collective-permute-start | bytes 393224 | tf_op jit(solution)/shard_map/ppermute | solution.py:30
  680.0 7.4 %collective-permute-start.23 = (bf16[2,16,2048]{2,1,0:T(8,128)(2,1)S(1)}, bf16[2,16,2048]{2,1,0:T(8,128)(2,1)S(1)}, u32[]{:S(2)}, u32[]{:S(2)}) collective-permute-start(bf16[2,16,2048]{2,1,0:T(8,128)(2,1)S(1)} %fusion.164), channel_id=1, source_target_pairs={{0,4},{1,5},{2,6},{3,7},{4,0},{5,1},{6,2},{7,3},{8,12},{9,13},{10,... | collective-permute-start | bytes 393224 | tf_op jit(solution)/shard_map/ppermute | solution.py:30
  682.7 5.3 collective-permute-start.29
  687.5 4.3 collective-permute-start.24
  (62 other events, 555.6 us)
Sparse Core Ops, SparseCore 0:
  16.6 80.8 all-gather.1

commit v2 on v0

v2 whole, which is shorter than its diff:
```python
import functools

import jax
import jax.numpy as jnp
from jax import lax
from jax.experimental import pallas as pl
from jax.experimental.pallas import tpu as pltpu
from jax.sharding import PartitionSpec as P

HEAD = 64
LANES = 128
FAR = -1e30
AXES = ("dp", "fsdp")
LOW = jnp.bfloat16
FULL = jnp.float32
ROOM = 56 << 20


def nn(left, right):
    return lax.dot_general(left, right, (((1,), (0,)), ((), ())), preferred_element_type=FULL)


def nt(left, right):
    return lax.dot_general(left, right, (((1,), (1,)), ((), ())), preferred_element_type=FULL)


def tn(left, right):
    return lax.dot_general(left, right, (((0,), (0,)), ((), ())), preferred_element_type=FULL)


def one_head(pair, odd):
    lane = lax.broadcasted_iota(jnp.int32, pair.shape, 1)
    return jnp.where((lane >= HEAD) == bool(odd), pair, jnp.zeros_like(pair))


def later_keys(rows, keys):
    query = lax.broadcasted_iota(jnp.int32, (rows, keys), 0)
    key = lax.broadcasted_iota(jnp.int32, (rows, keys), 1)
    return query, key


def call(body, name, grid, ins, outs, scratch=(), flops=0, moved=0, after=(), scalars=()):
    used = len(ins)

    def only_used(*refs):
        front = len(scalars)
        body(*refs[: front + used], *refs[front + used + len(after) :])

    def spec_of(spec):
        if not scalars or spec.index_map is None:
            return spec
        place = spec.index_map
        return pl.BlockSpec(
            spec.block_shape, lambda i, *_: place(i), pipeline_mode=spec.pipeline_mode
        )

    return pl.pallas_call(
        only_used if after else body,
        name=name,
        grid_spec=pltpu.PrefetchScalarGridSpec(
            num_scalar_prefetch=len(scalars),
            grid=(grid,),
            in_specs=[spec_of(spec) for _, spec in ins]
            + [pl.BlockSpec(memory_space=pl.ANY) for _ in after],
            out_specs=[spec_of(spec) for _, _, spec in outs],
            scratch_shapes=list(scratch),
        ),
        out_shape=[jax.ShapeDtypeStruct(shape, kind) for shape, kind, _ in outs],
        compiler_params=pltpu.CompilerParams(vmem_limit_bytes=ROOM),
        cost_estimate=pl.CostEstimate(flops=flops, bytes_accessed=moved, transcendentals=0),
    )(*scalars, *[array for array, _ in ins], *after)


def rows_of(block, columns):
    return pl.BlockSpec((block, columns), lambda i: (i, 0))


def fixed(shape, place=None):
    place = (0,) * len(shape) if place is None else place
    return pl.BlockSpec(shape, lambda i: place, pipeline_mode=pl.Buffered(1))


def all_of(array):
    return (array, fixed(array.shape))


def out_all(shape, kind):
    return (shape, kind, fixed(shape))


def attend(queries, hot, keys_ref, values_ref, count, causal):
    rows = queries.shape[0]
    pairs = queries.shape[1] // LANES
    lane = lax.broadcasted_iota(jnp.int32, (rows, LANES), 1)
    logs = jnp.zeros((rows, LANES), FULL)
    if causal:
        query, key = later_keys(rows, rows)
        ahead = jnp.where(key <= query, 0.0, FAR)
    mixed = []
    for pair in range(pairs):
        columns = slice(pair * LANES, (pair + 1) * LANES)
        total = None
        for odd in range(2):
            asked = jnp.concatenate([one_head(queries[:, columns], odd), hot], axis=1)
            spans = [(0, count)]
            if causal:
                spans = [(0, count - rows), (count - rows, count)]
                spans = [span for span in spans if span[0] < span[1]]
            scores = [nt(asked, keys_ref[pair, a:b, :]) for a, b in spans]
            if causal:
                scores[-1] = scores[-1] + ahead
            top = functools.reduce(
                jnp.maximum, [jnp.max(part, axis=1, keepdims=True) for part in scores]
            )
            weights = [jnp.exp(part - top) for part in scores]
            amount = sum(jnp.sum(part, axis=1, keepdims=True) for part in weights)
            share = 1.0 / amount
            heads = sum(
                nn((part * share).astype(LOW), values_ref[a:b, columns])
                for part, (a, b) in zip(weights, spans)
            )
            total = heads if total is None else jnp.where(lane < HEAD, total, heads)
            logs = jnp.where(lane == 2 * pair + odd, top + jnp.log(amount), logs)
        mixed.append(total)
    return jnp.concatenate(mixed, axis=1), logs.T[: 2 * pairs]


def keep_keys(keys_ref, place, keys, hot):
    pairs = keys.shape[1] // LANES
    for pair in range(pairs):
        keys_ref[pair, place, :LANES] = keys[:, pair * LANES : (pair + 1) * LANES]
        keys_ref[pair, place, LANES:] = hot


def self_forward(
    tokens, hot, far, gate, w_in, w_out, bias_columns, w_query,
    projected, mixed, logs, first, cross_queries, keys, values, bias,
):
    step = pl.program_id(0)
    rows, d = tokens.shape

    @pl.when(step == 0)
    def _():
        bias[...] = bias_columns[:, :LANES].astype(FULL).T[:8]

    joined_bias = jnp.concatenate([bias[0:1, :], jnp.zeros((1, d), FULL), bias[1:2, :]], axis=1)
    made = (nn(tokens[...], w_in[...]) + joined_bias).astype(LOW)
    projected[...] = made
    place = pl.ds(pl.multiple_of(step * rows, rows), rows)
    keep_keys(keys, place, made[:, d : 2 * d], far[...])
    values[place, :] = made[:, 2 * d :]
    for block in range(values.shape[0] // rows):

        @pl.when(step == block)
        def _(count=(block + 1) * rows):
            scaled = made[:, :d] * jnp.asarray(HEAD**-0.5, LOW)
            mixed[...], logs[...] = attend(scaled, hot[...], keys, values, count, True)

    branch = nt(mixed[...].astype(LOW), w_out[...]) + bias[2:3, :]
    total = tokens[...].astype(FULL) + gate[...] * branch
    first[...] = total
    cross_queries[...] = (nn(total.astype(LOW), w_query[...]) + bias[3:4, :]).astype(LOW)


def cross_forward(
    queries, memory, hot, far, gate, first, w_kv, w_out, bias_columns,
    memory_kv, mixed, logs, second, keys, bias,
):
    d = memory.shape[1]

    @pl.when(pl.program_id(0) == 0)
    def _():
        bias[...] = bias_columns[:, :LANES].astype(FULL).T[:8]
        made = nn(memory[...], w_kv[...])
        memory_kv[:, :d] = made[:, :d].astype(LOW)
        memory_kv[:, d:] = (made[:, d:] + bias[4:5, :]).astype(LOW)
        keep_keys(keys, slice(None), memory_kv[:, :d], far[...])

    scaled = queries[...] * jnp.asarray(HEAD**-0.5, LOW)
    mixed[...], logs[...] = attend(
        scaled, hot[...], keys, memory_kv.at[:, d:], memory.shape[0], False
    )
    branch = nt(mixed[...].astype(LOW), w_out[...]) + bias[5:6, :]
    second[...] = first[...] + gate[...] * branch


def head_sums(left, right):
    d = left.shape[1]
    head = lax.broadcasted_iota(jnp.int32, (d // HEAD, d), 0)
    column = lax.broadcasted_iota(jnp.int32, (d // HEAD, d), 1)
    chosen = (column // HEAD == head).astype(FULL)
    return lax.dot_general(
        chosen,
        left.astype(FULL) * right.astype(FULL),
        (((1,), (1,)), ((), ())),
        precision=lax.Precision.HIGHEST,
        preferred_element_type=FULL,
    )


def gelu_both(z):
    c = 0.7978845608028654
    square = z * z
    bent = jnp.tanh(c * z * (1.0 + 0.044715 * square))
    half = 0.5 * (1.0 + bent)
    slope = half + 0.5 * z * (1.0 - bent * bent) * (c * (1.0 + 3.0 * 0.044715 * square))
    return z * half, slope


def spread(d, ff):
    each = ff // d
    row = lax.broadcasted_iota(jnp.int32, (d, ff), 0)
    entry = lax.broadcasted_iota(jnp.int32, (d, ff), 1)
    column = lax.broadcasted_iota(jnp.int32, (LANES, ff), 0)
    there = lax.broadcasted_iota(jnp.int32, (LANES, ff), 1)
    return entry // each == row, (there % each == column).astype(LOW)


def columns_to_row(columns, ff):
    owner, place = spread(columns.shape[0], ff)
    return jnp.sum(jnp.where(owner, nn(columns, place), 0.0), axis=0, keepdims=True)


def row_to_columns(row, d):
    owner, place = spread(d, row.shape[1])
    return nt(jnp.where(owner, row, 0.0).astype(LOW), place).astype(LOW)


def rows_to_columns(*rows):
    d = rows[0].shape[1]
    stack = jnp.concatenate([*rows, jnp.zeros((LANES - len(rows), d), FULL)], axis=0)
    return stack.T.astype(LOW)


def feed_both(
    second, upstream, gate, mixed, w_in, w_out, w_cross_out, bias_columns,
    output, second_grad, cross_signal, mixed_grad, deltas, feed_grad, sums,
    second_low, signal_all, hidden_all, before_all, bias, bias_in, bias_in_grad,
):
    step = pl.program_id(0)
    rows, d = second.shape
    ff = w_in.shape[1]
    place = pl.ds(pl.multiple_of(step * rows, rows), rows)
    low = second[...].astype(LOW)
    second_low[place, :] = low
    given = upstream[...].astype(FULL)
    signal = (gate[...] * given).astype(LOW)
    signal_all[place, :] = signal

    @pl.when(step == 0)
    def _():
        bias[...] = bias_columns[:, :LANES].astype(FULL).T[:8]
        bias_in[...] = columns_to_row(bias_columns[:, LANES:], ff)
        bias_in_grad[...] = jnp.zeros_like(bias_in_grad)
        sums[...] = jnp.zeros_like(sums)

    made = bias[6:7, :]
    back = given


    width = 512
    for start in range(0, ff, width):
        part = slice(start, start + width)
        before = nn(low, w_in[:, part]) + bias_in[:, part]
        hidden, slope = gelu_both(before)
        hidden = hidden.astype(LOW)
        hidden_all[place, part] = hidden
        made = made + nt(hidden, w_out[:, part])
        before_grad = (nn(signal, w_out[:, part]) * slope).astype(LOW)
        before_all[place, part] = before_grad
        back = back + nt(before_grad, w_in[:, part])
        bias_in_grad[:, part] += jnp.sum(before_grad.astype(FULL), axis=0, keepdims=True)
    output[...] = (second[...] + gate[...] * made).astype(LOW)
    second_grad[...] = back
    crossed = (gate[...] * back).astype(LOW)
    cross_signal[...] = crossed
    mixed_back = nn(crossed, w_cross_out[...]).astype(LOW)
    mixed_grad[...] = mixed_back
    deltas[...] = head_sums(mixed_back, mixed[...])
    sums[0:1, :] += jnp.sum(signal.astype(FULL), axis=0, keepdims=True)
    sums[1:2, :] += jnp.sum(crossed.astype(FULL), axis=0, keepdims=True)

    @pl.when(step == pl.num_programs(0) - 1)
    def _():
        for start in range(0, ff, width):
            part = slice(start, start + width)
            feed_grad[:, part] = tn(second_low[...], before_all[:, part]).astype(LOW)
            feed_grad[:, ff + start : ff + start + width] = tn(
                signal_all[...], hidden_all[:, part]
            ).astype(LOW)
        feed_grad[:, 2 * ff : 2 * ff + LANES] = rows_to_columns(sums[0:1, :])
        feed_grad[:, 2 * ff + LANES :] = row_to_columns(bias_in_grad[...], d)


def attend_back(
    queries, keys, values, hot, far, mixed_grad, logs, deltas,
    query_grad, key_grad, value_grad, key_sum, value_sum, reached, *, causal, block, pair,
):
    count = keys.shape[0]
    reached[:, :LANES] = keys[...]
    reached[:, LANES:] = far[...]
    turned = keys[...].T
    if causal:
        key, query = later_keys(block, block)
        ahead = jnp.where(key <= query, 0.0, FAR)
    for start in range(queries.shape[0] - block, -1, -block):
        place = slice(start, start + block)
        spans = [(0, count)]
        if causal:
            spans = [(0, start), (start, start + block)]
            spans = [span for span in spans if span[0] < span[1]]
        first = start == queries.shape[0] - block
        grad = []
        for odd in range(2):
            head = 2 * pair + odd
            asked = one_head(queries[place, :], odd) * jnp.asarray(HEAD**-0.5, LOW)
            wanted = jnp.concatenate([asked, hot[place, :]], axis=1)
            incoming = one_head(mixed_grad[place, :], odd)
            turned_grad = None
            for a, b in spans:
                scores = nt(reached[a:b, :], wanted)
                if causal and b == start + block:
                    scores = scores + ahead
                chances = jnp.exp(scores - logs[head : head + 1, place])
                pushed = nt(values[a:b, :], incoming)
                score_grad = (chances * (pushed - deltas[head : head + 1, place])).astype(LOW)
                value_part = nn(chances.astype(LOW), incoming)
                key_part = nn(score_grad, asked)
                if first and odd == 0:
                    value_sum[a:b, :] = value_part
                    key_sum[a:b, :] = key_part
                else:
                    value_sum[a:b, :] += value_part
                    key_sum[a:b, :] += key_part
                part = nn(turned[odd * HEAD : (odd + 1) * HEAD, a:b], score_grad)
                turned_grad = part if turned_grad is None else turned_grad + part
            grad.append(turned_grad)
        both = jnp.concatenate(grad, axis=0) * HEAD**-0.5
        query_grad[place, :] = both.T.astype(LOW)
    key_grad[...] = key_sum[...].astype(LOW)
    value_grad[...] = value_sum[...].astype(LOW)


def back_of_pair(
    queries, keys, values, hot, far, mixed_grad, logs, deltas, pair, causal, at, after=()
):
    count = queries.shape[0]
    key_count = keys.shape[0]
    column = lambda rows, place: pl.BlockSpec((rows, LANES), lambda i: (0, place))
    whole = lambda array: fixed(array.shape)
    flops = 5 * 2 * count * key_count * LANES * 2 // (2 if causal else 1)
    return call(
        functools.partial(attend_back, causal=causal, block=256, pair=pair),
        "self_back" if causal else "cross_back",
        1,
        [
            (queries, column(count, at[0] + pair)),
            (keys, column(key_count, at[1] + pair)),
            (values, column(key_count, at[2] + pair)),
            (hot, whole(hot)),
            (far, whole(far)),
            (mixed_grad, column(count, pair)),
            (logs, whole(logs)),
            (deltas, whole(deltas)),
        ],
        [
            ((count, LANES), LOW, fixed((count, LANES))),
            ((key_count, LANES), LOW, fixed((key_count, LANES))),
            ((key_count, LANES), LOW, fixed((key_count, LANES))),
        ],
        [
            pltpu.VMEM((key_count, LANES), FULL),
            pltpu.VMEM((key_count, LANES), FULL),
            pltpu.VMEM((key_count, 2 * LANES), LOW),
        ],
        flops=flops,
        moved=8 << 18,
        after=after,
    )


def joined(refs):
    return jnp.concatenate([ref[...] for ref in refs], axis=1)


def column_sum(array):
    return jnp.sum(array.astype(FULL), axis=0, keepdims=True)


def part_by_core(bits, grads, keep, away):
    own = keep.shape[1]
    for core in range(2):

        @pl.when(bits[0] == core)
        def _(core=core):
            for slab in range(2 * keep.shape[0]):
                there = keep if slab % 2 == core else away
                there[slab // 2] = grads[slab * own : (slab + 1) * own, :]


def cross_joined(bits, *refs, pairs):
    parts, refs = refs[: 3 * pairs], refs[3 * pairs :]
    (
        first, second_grad, memory, cross_signal, cross_mixed, self_mixed, gate, w_query, w_out,
        sums, *outs,
    ) = refs
    *owned, first_grad, mixed_grad, deltas, grads = outs
    d = first.shape[1]
    query_signal = joined(parts[0::3])
    key_signal = joined(parts[1::3])
    value_signal = joined(parts[2::3])
    grads[:, :d] = tn(memory[...], key_signal).astype(LOW)
    grads[:, d : 2 * d] = tn(memory[...], value_signal).astype(LOW)
    grads[:, 2 * d : 3 * d] = tn(first[...].astype(LOW), query_signal).astype(LOW)
    grads[:, 3 * d : 4 * d] = tn(cross_signal[...], cross_mixed[...].astype(LOW)).astype(LOW)
    back = second_grad[...] + nt(query_signal, w_query[...])
    first_grad[...] = back
    signal = (gate[...] * back).astype(LOW)
    grads[:, 4 * d : 5 * d] = tn(signal, self_mixed[...].astype(LOW)).astype(LOW)
    grads[:, 5 * d :] = rows_to_columns(
        column_sum(query_signal), column_sum(value_signal), sums[1:2, :], column_sum(signal)
    )
    mixed_back = nn(signal, w_out[...]).astype(LOW)
    mixed_grad[...] = mixed_back
    deltas[...] = head_sums(mixed_back, self_mixed[...])
    if len(owned) == 2:
        part_by_core(bits, grads, *owned)
    else:
        owned[0][...] = grads[...]


def self_joined(bits, *refs, pairs):
    parts, (tokens, *owned, signal, grads) = refs[: 3 * pairs], refs[3 * pairs :]
    d = tokens.shape[1]
    added = []
    for which in range(3):
        part = joined(parts[which::3])
        signal[:, which * d : (which + 1) * d] = part
        grads[:, which * d : (which + 1) * d] = tn(tokens[...], part).astype(LOW)
        if which != 1:
            added.append(column_sum(part))
    grads[:, 3 * d :] = rows_to_columns(*added)
    if len(owned) == 2:
        part_by_core(bits, grads, *owned)
    else:
        owned[0][...] = grads[...]


def last_grads(*refs, pairs):
    parts = refs[: 2 * pairs]
    signal, first_grad, w_in, w_kv, tokens_grad, memory_grad = refs[2 * pairs :]
    d = w_in.shape[0]
    tokens_grad[...] = first_grad[...] + nt(signal[...], w_in[...])
    memory_grad[...] = nt(joined(parts[0::2]), w_kv[:, :d]) + nt(joined(parts[1::2]), w_kv[:, d:])


def sum_to_owners(grads, device_count, orders):
    me = lax.axis_index(AXES)
    bits = device_count.bit_length() - 1
    running = []
    for grad in grads:
        rows, columns = grad.shape
        running.append(grad.reshape((2,) * bits + (rows // device_count, columns)))
    left = [list(range(bits)) for _ in grads]
    for step in range(bits):
        sent = []
        for part, order in enumerate(orders):
            bit = order[step]
            axis = len(left[part]) - 1 - left[part].index(bit)
            mine = (me >> bit) & 1
            away = lax.dynamic_index_in_dim(running[part], 1 - mine, axis, keepdims=False)
            pairs = [(i, i ^ (1 << bit)) for i in range(device_count)]
            sent.append((axis, mine, lax.ppermute(away.astype(LOW), AXES, pairs)))
            left[part].remove(bit)
        for part, (axis, mine, got) in enumerate(sent):
            kept = lax.dynamic_index_in_dim(running[part], mine, axis, keepdims=False)
            running[part] = kept.astype(FULL) + got.astype(FULL)
    return running


def swap(array, bit, device_count):
    return lax.ppermute(array, AXES, [(i, i ^ (1 << bit)) for i in range(device_count)])


def scatter_rows(grad, device_count):
    bits = device_count.bit_length() - 1
    high = list(range(1, bits))[::-1]
    half = grad.shape[1] // 256 * 128
    orders = ([0] + high, [0, high[1], high[0]] + high[2:])
    return jnp.concatenate(
        sum_to_owners([grad[:, :half], grad[:, half:]], device_count, orders), axis=1
    )


def plus(kept, got):
    return kept.astype(FULL) + got.astype(FULL)


def fold_core(bits, keep, got, away_x, away_y, keep_x, keep_y):
    half = away_x.shape[-1]
    x, y = bits[3], bits[4]
    for y_place in range(2):
        left = lambda at: plus(keep[y_place, at, :, :, :, :half], got[y_place, at, :, :, :, :half])
        away_x[y_place] = left(1 - x).astype(LOW)
        keep_x[y_place] = left(x)
    for x_place in range(2):
        right = lambda at: plus(keep[at, x_place, :, :, :, half:], got[at, x_place, :, :, :, half:])
        away_y[x_place] = right(1 - y).astype(LOW)
        keep_y[x_place] = right(y)


def fold_plane(bits, keep_x, got_x, keep_y, got_y, away_y, away_x, next_y, next_x):
    x, y = bits[3], bits[4]
    away_y[...] = plus(keep_x[1 - y], got_x[1 - y]).astype(LOW)
    next_y[...] = plus(keep_x[y], got_x[y])
    away_x[...] = plus(keep_y[1 - x], got_y[1 - x]).astype(LOW)
    next_x[...] = plus(keep_y[x], got_y[x])


def fold_line(bits, keep_y, got_y, keep_x, got_x, away, keep):
    half = keep_y.shape[-1]
    z = bits[1]
    for place in range(2):
        away[place, :, :half] = plus(keep_y[place, 1 - z], got_y[place, 1 - z]).astype(LOW)
        away[place, :, half:] = plus(keep_x[place, 1 - z], got_x[place, 1 - z]).astype(LOW)
        keep[place, :, :half] = plus(keep_y[place, z], got_y[place, z])
        keep[place, :, half:] = plus(keep_x[place, z], got_x[place, z])


def fold_ends(bits, keep, got, away, last):
    z = bits[2]
    away[...] = plus(keep[1 - z], got[1 - z]).astype(LOW)
    last[...] = plus(keep[z], got[z])


class Halving:
    def __init__(self, name, bits, keep, away, half, device_count):
        self.name, self.bits, self.half, self.device_count = name, bits, half, device_count
        self.own, self.columns = keep.shape[-2:]
        shape = (2, 2, 2, 2, self.own, self.columns)
        self.kept = [keep.reshape(shape)]
        self.sent = [away.reshape(shape)]
        self.got = self.send(0)

    def send(self, *order):
        return [swap(array, bit, self.device_count) for array, bit in zip(self.sent, order)]

    def fold(self, body, step, outs, *order):
        ins = [all_of(part) for pair in zip(self.kept, self.got) for part in pair]
        made = call(
            body, self.name + step, 1, ins, [out_all(*out) for out in outs],
            scalars=(self.bits,), after=self.after,
        )
        count = len(made) // 2
        self.sent, self.kept = made[:count], made[count:]
        self.got = self.send(*order)

    def step(self, number, after=()):
        self.after = tuple(after)
        own, half, rest = self.own, self.half, self.columns - self.half
        if number == 1:
            left, right = (2, 2, 2, own, half), (2, 2, 2, own, rest)
            outs = [(left, LOW), (right, LOW), (left, FULL), (right, FULL)]
            self.fold(fold_core, "_core", outs, 3, 4)
        if number == 2:
            left, right = (2, 2, own, half), (2, 2, own, rest)
            outs = [(left, LOW), (right, LOW), (left, FULL), (right, FULL)]
            self.fold(fold_plane, "_plane", outs, 4, 3)
        if number == 3:
            both = (2, own, self.columns)
            self.fold(fold_line, "_line", [(both, LOW), (both, FULL)], 1)
        if number == 4:
            both = (own, self.columns)
            self.fold(fold_ends, "_ends", [(both, LOW), (both, FULL)], 2)


def cross_last(keep, got, kv, query, cross_out, self_out, cross_bias, self_bias):
    total = plus(keep[...], got[...])
    d = query.shape[1]
    kv[...] = total[:, : 2 * d]
    query[...] = total[:, 2 * d : 3 * d]
    cross_out[...] = total[:, 3 * d : 4 * d]
    self_out[...] = total[:, 4 * d : 5 * d]
    turned = turned_bias(total[:, 5 * d :])
    cross_bias[...] = turned[0:3]
    self_bias[...] = turned[3:4]


def turned_bias(columns):
    own = columns.shape[0]
    square = jnp.concatenate([columns, jnp.zeros((LANES - own, LANES), FULL)], axis=0)
    return square.T[:8, :own]


def self_last(keep, got, third, self_in, bias):
    total = plus(keep[...], got[...])
    columns = self_in.shape[1]
    self_in[...] = total[:, :columns]
    bias[0:2, :] = turned_bias(total[:, columns:])[0:2]
    bias[2:3, :] = third[...]


def feed_last(total, feed_in, feed_out, bias_out, bias_in):
    ff = feed_in.shape[1]
    feed_in[...] = total[:, :ff].astype(FULL)
    feed_out[...] = total[:, ff : 2 * ff].astype(FULL)
    bias_out[...] = turned_bias(total[:, 2 * ff : 2 * ff + LANES].astype(FULL))[0:1]
    bias_in[...] = total[:, 2 * ff + LANES :].astype(FULL)


def pack(
    self_in, self_out, cross_query, cross_kv, cross_out, feed_in, feed_out, self_bias, cross_bias,
    bias_out, bias_in, own_self, own_cross, own_feed,
):
    d = self_out.shape[1]
    ff = feed_in.shape[1]
    own = self_in.shape[0]
    own_self[:, : 3 * d] = self_in[...].astype(LOW)
    own_self[:, 3 * d : 4 * d] = self_out[...].astype(LOW)
    rows = jnp.concatenate(
        [self_bias[...], cross_bias[...], bias_out[...], jnp.zeros((LANES - 7, own), FULL)], axis=0
    )
    wide = jnp.concatenate([rows, jnp.zeros((LANES, LANES - own), FULL)], axis=1)
    own_self[:, 4 * d : 4 * d + LANES] = wide.T[:own].astype(LOW)
    own_self[:, 4 * d + LANES :] = jnp.zeros((own, LANES), LOW)
    own_self[:, 4 * d + LANES : 4 * d + LANES + ff // d] = bias_in[...].astype(LOW)
    own_cross[:, : 2 * d] = cross_kv[...].astype(LOW)
    own_cross[:, 2 * d : 3 * d] = cross_query[...].astype(LOW)
    own_cross[:, 3 * d :] = cross_out[...].astype(LOW)
    own_feed[:, :ff] = feed_in[...].astype(LOW)
    own_feed[:, ff:] = feed_out[...].astype(LOW)


def gather_halves(left, right, device_count):
    me = lax.axis_index(AXES)
    held = [left, right]
    known = [[], []]
    for bits in ((2, 2), (1, 1), (3, 4), (4, 3), (0, 0)):
        got = [swap(array, bit, device_count) for array, bit in zip(held, bits)]
        for part, bit in enumerate(bits):
            axis = sum(other > bit for other in known[part])
            low = jnp.stack([held[part], got[part]], axis)
            high = jnp.stack([got[part], held[part]], axis)
            held[part] = jnp.where((me >> bit) & 1, high, low)
            known[part].append(bit)
    return [array.reshape(-1, array.shape[-1]) for array in held]


def numbered(lengths, positions, padding):
    boundary = jnp.cumsum(lengths, dtype=jnp.int32)
    position = lax.broadcasted_iota(jnp.int32, (positions, 1), 0)
    number = jnp.sum((position >= boundary[None, :]).astype(jnp.int32), axis=1, keepdims=True)
    present = position < boundary[-1]
    return jnp.where(present, number, padding), present


def on_device(
    tokens, memory, out_cotangent, seq_lengths, memory_lengths, residual_gate,
    self_in, self_out, self_bias, cross_query, cross_key_value, cross_out, cross_bias,
    feed_in, feed_out, feed_bias_in, feed_bias_out,
):
    device_count = lax.axis_size(AXES)
    count, d = tokens.shape
    key_count = memory.shape[0]
    ff = feed_in.shape[1]
    own = self_in.shape[0]
    pairs = d // LANES
    heads = d // HEAD
    block = 256
    steps = count // block
    halving = lax.axis_size("dp") == 4 and lax.axis_size("fsdp") == 8
    me = lax.axis_index(AXES)
    bits = jnp.stack([(me >> bit) & 1 for bit in range(5)]).astype(jnp.int32)
    own_self, own_cross, own_feed = call(
        pack,
        "pack",
        1,
        [
            all_of(array)
            for array in (
                self_in, self_out.T, cross_query, cross_key_value, cross_out.T, feed_in,
                feed_out.T, self_bias, cross_bias, feed_bias_out[None], feed_bias_in.reshape(own, -1),
            )
        ],
        [
            out_all((own, 4 * d + 2 * LANES), LOW),
            out_all((own, 4 * d), LOW),
            out_all((own, 2 * ff), LOW),
        ],
    )
    feed_whole = lax.all_gather(own_feed, AXES, axis=0, tiled=True)
    if halving:
        self_whole, cross_whole = gather_halves(own_self, own_cross, device_count)
    else:
        self_whole = lax.all_gather(own_self, AXES, axis=0, tiled=True)
        cross_whole = lax.all_gather(own_cross, AXES, axis=0, tiled=True)
    w_self_in = (self_whole, fixed((d, 3 * d), (0, 0)))
    w_self_out = (self_whole, fixed((d, d), (0, 3)))
    bias_columns = (self_whole, fixed((d, 2 * LANES), (0, 4 * d // (2 * LANES))))
    w_kv = (cross_whole, fixed((d, 2 * d), (0, 0)))
    w_query = (cross_whole, fixed((d, d), (0, 2)))
    w_cross_out = (cross_whole, fixed((d, d), (0, 3)))
    w_feed_in = (feed_whole, fixed((d, ff), (0, 0)))
    w_feed_out = (feed_whole, fixed((d, ff), (0, 1)))

    slots = seq_lengths.shape[1]
    query_ids, present = numbered(seq_lengths[0], count, slots)
    memory_ids, _ = numbered(memory_lengths[0], key_count, slots + 1)
    lanes = lax.broadcasted_iota(jnp.int32, (1, LANES), 1)
    hot = (query_ids == lanes).astype(LOW)
    self_far = jnp.where(query_ids == lanes, 0.0, FAR).astype(LOW)
    memory_far = jnp.where(memory_ids == lanes, 0.0, FAR).astype(LOW)
    gate = residual_gate[0] * present.astype(FULL)

    each = lambda array: (array, rows_of(block, array.shape[1]))
    out_rows = lambda columns, kind: ((count, columns), kind, rows_of(block, columns))
    out_heads = ((heads, count), FULL, pl.BlockSpec((heads, block), lambda i: (0, i)))

    projected, self_mixed, self_logs, first, cross_queries = call(
        self_forward,
        "self_forward",
        steps,
        [each(tokens), each(hot), each(self_far), each(gate), w_self_in, w_self_out, bias_columns,
         w_query],
        [out_rows(3 * d, LOW), out_rows(d, FULL), out_heads, out_rows(d, FULL), out_rows(d, LOW)],
        [pltpu.VMEM((pairs, count, 2 * LANES), LOW), pltpu.VMEM((count, d), LOW),
         pltpu.VMEM((8, d), FULL)],
        flops=15 << 30, moved=8 << 20,
    )
    memory_kv, cross_mixed, cross_logs, second = call(
        cross_forward,
        "cross_forward",
        steps,
        [each(cross_queries), all_of(memory), each(hot), all_of(memory_far), each(gate),
         each(first), w_kv, w_cross_out, bias_columns],
        [out_all((key_count, 2 * d), LOW), out_rows(d, FULL), out_heads, out_rows(d, FULL)],
        [pltpu.VMEM((pairs, key_count, 2 * LANES), LOW), pltpu.VMEM((8, d), FULL)],
        flops=20 << 30, moved=8 << 20,
    )
    output, second_grad, cross_signal, cross_mixed_grad, cross_deltas, feed_grad, feed_sums = call(
        feed_both,
        "feed_both",
        steps,
        [each(second), each(out_cotangent), each(gate), each(cross_mixed), w_feed_in, w_feed_out,
         w_cross_out, bias_columns],
        [out_rows(d, LOW), out_rows(d, FULL), out_rows(d, LOW), out_rows(d, LOW), out_heads,
         out_all((d, 2 * ff + 2 * LANES), LOW), out_all((8, d), FULL)],
        [pltpu.VMEM((count, d), LOW), pltpu.VMEM((count, d), LOW), pltpu.VMEM((count, ff), LOW),
         pltpu.VMEM((count, ff), LOW), pltpu.VMEM((8, d), FULL), pltpu.VMEM((1, ff), FULL),
         pltpu.VMEM((1, ff), FULL)],
        flops=25 << 30, moved=16 << 20,
    )
    feed_total = lax.psum_scatter(feed_grad, "dp", scatter_dimension=0, tiled=True)
    feed_total = lax.psum_scatter(feed_total, "fsdp", scatter_dimension=0, tiled=True)

    cross_parts = []
    for pair in range(pairs):
        cross_parts += back_of_pair(
            cross_queries, memory_kv, memory_kv, hot, memory_far, cross_mixed_grad, cross_logs,
            cross_deltas, pair, False, (0, 0, pairs),
        )

    def owned(columns):
        if halving:
            return [out_all((device_count // 2, own, columns), LOW)] * 2
        return [out_all((d, columns), LOW)]

    cross_columns = 5 * d + LANES
    *cross_owned, first_grad, self_mixed_grad, self_deltas = call(
        functools.partial(cross_joined, pairs=pairs),
        "cross_joined",
        1,
        [all_of(part) for part in cross_parts]
        + [all_of(first), all_of(second_grad), all_of(memory), all_of(cross_signal),
           all_of(cross_mixed), all_of(self_mixed), all_of(gate), w_query, w_self_out,
           all_of(feed_sums)],
        owned(cross_columns)
        + [out_all((count, d), FULL), out_all((count, d), LOW), out_all((heads, count), FULL)],
        [pltpu.VMEM((d, cross_columns), LOW)],
        flops=8 << 30, moved=16 << 20, scalars=(bits,),
    )
    if halving:
        cross_sum = Halving("cross_sum", bits, *cross_owned, 11 * LANES, device_count)

    self_parts = []
    for pair in range(pairs):
        after = ()
        if halving and pair:
            after = tuple(cross_sum.got)
            cross_sum.step(pair, self_parts[-1:])
        self_parts += back_of_pair(
            projected, projected, projected, hot, self_far, self_mixed_grad, self_logs,
            self_deltas, pair, True, (0, pairs, 2 * pairs), after,
        )
    after = ()
    if halving:
        after = tuple(cross_sum.got)
        cross_sum.step(4, self_parts[-1:])
    self_columns = 3 * d + LANES
    *self_owned, self_signal = call(
        functools.partial(self_joined, pairs=pairs),
        "self_joined",
        1,
        [all_of(part) for part in self_parts] + [all_of(tokens)],
        owned(self_columns) + [out_all((count, 3 * d), LOW)],
        [pltpu.VMEM((d, self_columns), LOW)],
        flops=2 << 30, moved=8 << 20, scalars=(bits,), after=after,
    )
    if halving:
        self_sum = Halving("self_sum", bits, *self_owned, 6 * LANES, device_count)
        ends = [(cross_sum.kept[0], cross_sum.got[0])]
        for number in range(1, 5):
            self_sum.step(number)
        ends.append((self_sum.kept[0], self_sum.got[0]))
    else:
        ends = []
        for grads in (cross_owned[0], self_owned[0]):
            total = scatter_rows(grads, device_count)
            ends.append((total, jnp.zeros_like(total)))
    tokens_grad, memory_grad = call(
        functools.partial(last_grads, pairs=pairs),
        "last_grads",
        1,
        [all_of(part) for index, part in enumerate(cross_parts) if index % 3]
        + [all_of(self_signal), all_of(first_grad), w_self_in, w_kv],
        [out_all((count, d), FULL), out_all((key_count, d), FULL)],
        flops=3 << 30, moved=12 << 20,
    )
    kv_grad, query_grad, cross_out_grad, self_out_grad, cross_bias_grad, third = call(
        cross_last, "cross_last", 1, [all_of(array) for array in ends[0]],
        [out_all((own, 2 * d), FULL), out_all((own, d), FULL), out_all((own, d), FULL),
         out_all((own, d), FULL), out_all((3, own), FULL), out_all((1, own), FULL)],
    )
    feed_in_grad, feed_out_grad, bias_out_grad, bias_in_grad = call(
        feed_last, "feed_last", 1, [all_of(feed_total)],
        [out_all((own, ff), FULL), out_all((own, ff), FULL), out_all((1, own), FULL),
         out_all((own, LANES), FULL)],
    )
    self_in_grad, self_bias_grad = call(
        self_last, "self_last", 1, [all_of(array) for array in (*ends[1], third)],
        [out_all((own, 3 * d), FULL), out_all((3, own), FULL)],
    )
    return (
        output,
        tokens_grad,
        memory_grad,
        self_in_grad,
        self_out_grad.T,
        self_bias_grad,
        query_grad,
        kv_grad,
        cross_out_grad.T,
        cross_bias_grad,
        feed_in_grad,
        feed_out_grad.T,
        bias_in_grad[:, : ff // d].reshape(feed_bias_in.shape),
        bias_out_grad[0],
    )


def solution(mesh):
    return jax.shard_map(
        on_device,
        mesh=mesh,
        in_specs=(
            P(("dp", "fsdp"), None),
            P(("dp", "fsdp"), None),
            P(("dp", "fsdp"), None),
            P(("dp", "fsdp"), None),
            P(("dp", "fsdp"), None),
            P(),
            P(("dp", "fsdp"), None),
            P(None, ("dp", "fsdp")),
            P(None, ("dp", "fsdp")),
            P(("dp", "fsdp"), None),
            P(("dp", "fsdp"), None),
            P(None, ("dp", "fsdp")),
            P(None, ("dp", "fsdp")),
            P(("dp", "fsdp"), None),
            P(None, ("dp", "fsdp")),
            P(("dp", "fsdp")),
            P(("dp", "fsdp")),
        ),
        out_specs=(
            P(("dp", "fsdp"), None),
            P(("dp", "fsdp"), None),
            P(("dp", "fsdp"), None),
            P(("dp", "fsdp"), None),
            P(None, ("dp", "fsdp")),
            P(None, ("dp", "fsdp")),
            P(("dp", "fsdp"), None),
            P(("dp", "fsdp"), None),
            P(None, ("dp", "fsdp")),
            P(None, ("dp", "fsdp")),
            P(("dp", "fsdp"), None),
            P(None, ("dp", "fsdp")),
            P(("dp", "fsdp")),
            P(("dp", "fsdp")),
        ),
        check_vma=False,
    )
```

time: 1930 us -> 310 us (0.16)
  waiting for transfers between devices: 1090 us -> 38.6 us
  matrix products: 385 us -> 0 us
  blocking collectives: 286 us -> 0 us
  Pallas kernels: 0 us -> 195 us
  local copies, waits for them, and re-layouts: 98.2 us -> 16.3 us
  other arithmetic: 48.6 us -> 10 us
  starting transfers between devices: 0.79 us -> 30.5 us
    reduce_scatter x5 -> x2, waiting for transfers between devices: 684 us -> 0.01 us  [the longest x1 0.01 us: on_device(): lax.psum_scatter(feed_grad, 'dp', scatter_dimension=0, tiled=True)]
    unnamed x17 -> x3, waiting for transfers between devices: 408 us -> 0.05 us
    dot_general x49 -> x0, matrix products: 385 us -> none  [the longest x4 94.8 us: per_block(): jnp.einsum('hqk,qhd->khd', score_grad, query_block, preferred_element_typ...]
    all_gather x5 -> x0, blocking collectives: 205 us -> none  [the longest x1 43.7 us: on_device(): lax.all_gather(cross_out.astype(low_type), ('dp', 'fsdp'), axis=1, tiled=...]
    pallas_call x0 -> x26, Pallas kernels: none -> 195 us  [call(): pl.pallas_call(only_used if after else body, name=name, grid_spec=pltpu.P...]
    unnamed x2 -> x0, blocking collectives: 80.6 us -> none
    ppermute x0 -> x24, waiting for transfers between devices: none -> 38.5 us  [swap(): lax.ppermute(array, AXES, [(i, i ^ 1 << bit) for i in range(device_count)])]
    while x28 -> x0, local copies, waits for them, and re-layouts: 36.8 us -> none  [the longest x4 26 us: attend_forward(): mixed_heads, log_totals = lax.map(per_block, (shaped, id_blocks, starts))]
  transfers between devices with their start and end apart: 13 -> 27, of which waited for: 9 -> 11; matrix products, arithmetic and copies ran while one was open for 10% -> 5% of each run, Pallas kernels for 0% -> 53%
where the time goes in v2:
time: 310 us; the launch traced here: 306 us
  Pallas kernels  195 us (63%)
  waiting for transfers between devices  38.6 us (12%)
  starting transfers between devices  30.5 us (10%)
  local copies, waits for them, and re-layouts  16.3 us (5%)
  between operations  14.9 us (5%)
  other arithmetic  10 us (3%)
    pallas_call x26, Pallas kernels, call(): pl.pallas_call(only_used if after else body, name=name, grid_spec=pltpu.P...  195 us
    ppermute x24, waiting for transfers between devices, swap(): lax.ppermute(array, AXES, [(i, i ^ 1 << bit) for i in range(device_count)])  38.5 us
    ppermute x24, starting transfers between devices, swap(): lax.ppermute(array, AXES, [(i, i ^ 1 << bit) for i in range(device_count)])  30.2 us
    unnamed x30, local copies, waits for them, and re-layouts  7.44 us
  transfers between devices with their start and end apart: 27, of which 11 were waited for; matrix products, arithmetic and copies ran while one was open for 5% of the time, Pallas kernels for 53%

profile of v2, /device:TPU:0, one launch (start us, length us, event | category | flops | bytes accessed | tf_op | source)
XLA Modules:
  0.0 305.5 jit_solution(7788516590748308065)
XLA Ops:
  10.5 4.1 %collective-permute-start.5 = (bf16[16,2048]{1,0:T(8,128)(2,1)}, bf16[16,2048]{1,0:T(8,128)(2,1)S(1)}, u32[]{:S(2)}, u32[]{:S(2)}) collective-permute-start(bf16[16,2048]{1,0:T(8,128)(2,1)} %get-tuple-element.104), channel_id=1, source_target_pairs={{0,4},{1,5},{2,6},{3,7},{4,0},{5,1},{6,2},{7,3},{8,12},{9,13},{10,... | collective-permute-start | bytes 196616 | tf_op jit(solution)/shard_map/ppermute | solution.py:482
  24.8 1.9 collective-permute-start.6
  28.0 4.0 %collective-permute-done.6 = bf16[2,16,2048]{2,1,0:T(8,128)(2,1)S(1)} collective-permute-done((bf16[2,16,2048]{2,1,0:T(8,128)(2,1)S(1)}, bf16[2,16,2048]{2,1,0:T(8,128)(2,1)S(1)}, u32[]{:S(2)}, u32[]{:S(2)}) %collective-permute-start.6) | collective-permute-done | bytes 131104 | tf_op jit(solution)/shard_map/ppermute | solution.py:482
  40.3 7.9 %collective-permute-done.2 = bf16[2,2,16,2304]{3,2,0,1:T(8,128)(2,1)S(1)} collective-permute-done((bf16[2,2,16,2304]{3,2,0,1:T(8,128)(2,1)S(1)}, bf16[2,2,16,2304]{3,2,0,1:T(8,128)(2,1)S(1)}, u32[]{:S(2)}, u32[]{:S(2)}) %collective-permute-start.2) | collective-permute-done | bytes 294944 | tf_op jit(solution)/shard_map/ppermute | solution.py:482
  49.9 8.0 %collective-permute-done.8 = bf16[2,2,2,16,2048]{4,3,1,2,0:T(8,128)(2,1)S(1)} collective-permute-done((bf16[2,2,2,16,2048]{4,3,1,2,0:T(8,128)(2,1)S(1)}, bf16[2,2,2,16,2048]{4,3,1,2,0:T(8,128)(2,1)S(1)}, u32[]{:S(2)}, u32[]{:S(2)}) %collective-permute-start.8) | collective-permute-done | bytes 524320 | tf_op jit(solution)/shard_map/ppermute | solution.py:482
  64.7 22.4 %self_forward.1 = (bf16[1024,1536]{1,0:T(8,128)(2,1)}, f32[1024,512]{1,0:T(8,128)}, f32[8,1024]{1,0:T(8,128)}, f32[1024,512]{1,0:T(8,128)}, bf16[1024,512]{1,0:T(8,128)(2,1)}) custom-call(bf16[1024,512]{1,0:T(8,128)(2,1)} %refs_13_.1, bf16[1024,128]{1,0:T(8,128)(2,1)} %fusion.hot.refs_3_, bf16[1024,128]{1,0:T(8,128)(2,1)} %select_convert_fusion.1.far.refs_4_, ...), custom_call_target="tpu_custom_call" | custom-call | flops 16106127360 | bytes 8388608 | tf_op jit(solution)/shard_map/self_forward/pallas_call | solution.py:57
  87.2 26.3 %cross_forward.1 = (bf16[1024,1024]{1,0:T(8,128)(2,1)}, f32[1024,512]{1,0:T(8,128)}, f32[8,1024]{1,0:T(8,128)}, f32[1024,512]{1,0:T(8,128)}) custom-call(bf16[1024,512]{1,0:T(8,128)(2,1)} %get-tuple-element.105.queries, bf16[1024,512]{1,0:T(8,128)(2,1)} %refs_14_.1, bf16[1024,128]{1,0:T(8,128)(2,1)} %fusion.hot.refs_3_, ...), custom_call_target="tpu_custom_call" | custom-call | flops 21474836480 | bytes 8388608 | tf_op jit(solution)/shard_map/cross_forward/pallas_call | solution.py:57
  113.5 30.2 %feed_both.1 = (bf16[1024,512]{1,0:T(8,128)(2,1)}, f32[1024,512]{1,0:T(8,128)}, bf16[1024,512]{1,0:T(8,128)(2,1)}, bf16[1024,512]{1,0:T(8,128)(2,1)}, f32[8,1024...) custom-call(f32[1024,512]{1,0:T(8,128)} %get-tuple-element.107.second, bf16[1024,512]{1,0:T(8,128)(2,1)} %upstream.1, ...), custom_call_target="tpu_custom_call" | custom-call | flops 26843545600 | bytes 16777216 | tf_op jit(solution)/shard_map/feed_both/pallas_call | solution.py:57
  144.6 7.6 %cross_back.7 = (bf16[1024,128]{1,0:T(8,128)(2,1)}, bf16[1024,128]{1,0:T(8,128)(2,1)}, bf16[1024,128]{1,0:T(8,128)(2,1)}) custom-call(bf16[1024,512]{1,0:T(8,128)(2,1)} %get-tuple-element.105.queries, bf16[1024,1024]{1,0:T(8,128)(2,1)} %get-tuple-element.111.keys.values, bf16[1024,1024]{1,0:T(8,128)(2,1)} %get-tuple-element.111.keys.values, ...), custom_call_target="tpu_custom_call" | custom-call | flops 2684354560 | bytes 2097152 | tf_op jit(solution)/shard_map/cross_back/pallas_call | solution.py:57
  152.2 7.5 %cross_back.6 = (bf16[1024,128]{1,0:T(8,128)(2,1)}, bf16[1024,128]{1,0:T(8,128)(2,1)}, bf16[1024,128]{1,0:T(8,128)(2,1)}) custom-call(bf16[1024,512]{1,0:T(8,128)(2,1)} %get-tuple-element.105.queries, bf16[1024,1024]{1,0:T(8,128)(2,1)} %get-tuple-element.111.keys.values, bf16[1024,1024]{1,0:T(8,128)(2,1)} %get-tuple-element.111.keys.values, ...), custom_call_target="tpu_custom_call" | custom-call | flops 2684354560 | bytes 2097152 | tf_op jit(solution)/shard_map/cross_back/pallas_call | solution.py:57
  159.7 7.9 %cross_back.5 = (bf16[1024,128]{1,0:T(8,128)(2,1)}, bf16[1024,128]{1,0:T(8,128)(2,1)}, bf16[1024,128]{1,0:T(8,128)(2,1)}) custom-call(bf16[1024,512]{1,0:T(8,128)(2,1)} %get-tuple-element.105.queries, bf16[1024,1024]{1,0:T(8,128)(2,1)} %get-tuple-element.111.keys.values, bf16[1024,1024]{1,0:T(8,128)(2,1)} %get-tuple-element.111.keys.values, ...), custom_call_target="tpu_custom_call" | custom-call | flops 2684354560 | bytes 2097152 | tf_op jit(solution)/shard_map/cross_back/pallas_call | solution.py:57
  167.6 7.6 %cross_back.4 = (bf16[1024,128]{1,0:T(8,128)(2,1)}, bf16[1024,128]{1,0:T(8,128)(2,1)}, bf16[1024,128]{1,0:T(8,128)(2,1)}) custom-call(bf16[1024,512]{1,0:T(8,128)(2,1)} %get-tuple-element.105.queries, bf16[1024,1024]{1,0:T(8,128)(2,1)} %get-tuple-element.111.keys.values, bf16[1024,1024]{1,0:T(8,128)(2,1)} %get-tuple-element.111.keys.values, ...), custom_call_target="tpu_custom_call" | custom-call | flops 2684354560 | bytes 2097152 | tf_op jit(solution)/shard_map/cross_back/pallas_call | solution.py:57
  175.2 14.7 %cross_joined.1 = (bf16[16,16,2688]{2,1,0:T(8,128)(2,1)}, bf16[16,16,2688]{2,1,0:T(8,128)(2,1)}, f32[1024,512]{1,0:T(8,128)}, bf16[1024,512]{1,0:T(8,128)(2,1)}, f32[8,1024]{1,0:T(8,128)}) custom-call(s32[5]{0:T(128)} %stack.275.bits.refs_0_, bf16[1024,128]{1,0:T(8,128)(2,1)} %get-tuple-element.124.refs_0_, ...), custom_call_target="tpu_custom_call" | custom-call | flops 8589934592 | bytes 16777216 | tf_op jit(solution)/shard_map/cross_joined/pallas_call | solution.py:57
  190.4 6.4 %self_back.4 = (bf16[1024,128]{1,0:T(8,128)(2,1)}, bf16[1024,128]{1,0:T(8,128)(2,1)}, bf16[1024,128]{1,0:T(8,128)(2,1)}) custom-call(bf16[1024,1536]{1,0:T(8,128)(2,1)} %get-tuple-element.123.queries.keys.values.refs_0_.refs_1_.refs_2_, bf16[1024,1536]{1,0:T(8,128)(2,1)} %get-tuple-element.123.queries.keys.values.refs_0_.refs_1_.refs_2_, ...), custom_call_target="tpu_custom_call" | custom-call | flops 1342177280 | bytes 2097152 | tf_op jit(solution)/shard_map/self_back/pallas_call | solution.py:57
  197.9 3.9 %cross_sum_core.1 = (bf16[2,2,2,16,1408]{4,3,2,1,0:T(8,128)(2,1)}, bf16[2,2,2,16,1280]{4,3,2,1,0:T(8,128)(2,1)}, f32[2,2,2,16,1408]{4,3,2,1,0:T(8,128)}, f32[2,2,2,16,1280]{4,3,2,1,0:T(8,128)}) custom-call(s32[5]{0:T(128)} %stack.275.bits.refs_0_, bf16[2,2,2,2,16,2688]{5,4,3,2,1,0:T(8,128)(2,1)} %bitcast.86, bf16[2,2,2,2,16,2688]{5,4,3,2,1,0:T(8,128)(2,1)} %copy-done, ...), custom_call_target="tpu_custom_call" | custom-call | tf_op jit(solution)/shard_map/cross_sum_core/pallas_call | solution.py:57
  204.8 6.4 %self_back.5 = (bf16[1024,128]{1,0:T(8,128)(2,1)}, bf16[1024,128]{1,0:T(8,128)(2,1)}, bf16[1024,128]{1,0:T(8,128)(2,1)}) custom-call(bf16[1024,1536]{1,0:T(8,128)(2,1)} %get-tuple-element.123.queries.keys.values.refs_0_.refs_1_.refs_2_, bf16[1024,1536]{1,0:T(8,128)(2,1)} %get-tuple-element.123.queries.keys.values.refs_0_.refs_1_.refs_2_, ...), custom_call_target="tpu_custom_call" | custom-call | flops 1342177280 | bytes 2097152 | tf_op jit(solution)/shard_map/self_back/pallas_call | solution.py:57
  213.8 3.2 %cross_sum_plane.1 = (bf16[2,2,16,1408]{3,2,1,0:T(8,128)(2,1)}, bf16[2,2,16,1280]{3,2,1,0:T(8,128)(2,1)}, f32[2,2,16,1408]{3,2,1,0:T(8,128)}, f32[2,2,16,1280]{3,2,1,0:T(8,128)}) custom-call(s32[5]{0:T(128)} %stack.275.bits.refs_0_, f32[2,2,2,16,1408]{4,3,2,1,0:T(8,128)} %get-tuple-element.148.refs_1_, bf16[2,2,2,16,1408]{4,3,2,1,0:T(8,128)(2,1)} %copy-done.1, ...), custom_call_target="tpu_custom_call" | custom-call | tf_op jit(solution)/shard_map/cross_sum_plane/pallas_call | solution.py:57
  219.6 6.6 %self_back.6 = (bf16[1024,128]{1,0:T(8,128)(2,1)}, bf16[1024,128]{1,0:T(8,128)(2,1)}, bf16[1024,128]{1,0:T(8,128)(2,1)}) custom-call(bf16[1024,1536]{1,0:T(8,128)(2,1)} %get-tuple-element.123.queries.keys.values.refs_0_.refs_1_.refs_2_, bf16[1024,1536]{1,0:T(8,128)(2,1)} %get-tuple-element.123.queries.keys.values.refs_0_.refs_1_.refs_2_, ...), custom_call_target="tpu_custom_call" | custom-call | flops 1342177280 | bytes 2097152 | tf_op jit(solution)/shard_map/self_back/pallas_call | solution.py:57
  226.9 2.7 cross_sum_line.1
  230.5 6.4 %self_back.7 = (bf16[1024,128]{1,0:T(8,128)(2,1)}, bf16[1024,128]{1,0:T(8,128)(2,1)}, bf16[1024,128]{1,0:T(8,128)(2,1)}) custom-call(bf16[1024,1536]{1,0:T(8,128)(2,1)} %get-tuple-element.123.queries.keys.values.refs_0_.refs_1_.refs_2_, bf16[1024,1536]{1,0:T(8,128)(2,1)} %get-tuple-element.123.queries.keys.values.refs_0_.refs_1_.refs_2_, ...), custom_call_target="tpu_custom_call" | custom-call | flops 1342177280 | bytes 2097152 | tf_op jit(solution)/shard_map/self_back/pallas_call | solution.py:57
  237.6 7.1 %self_joined.1 = (bf16[16,16,1664]{2,1,0:T(8,128)(2,1)}, bf16[16,16,1664]{2,1,0:T(8,128)(2,1)}, bf16[1024,1536]{1,0:T(8,128)(2,1)}) custom-call(s32[5]{0:T(128)} %stack.275.bits.refs_0_, bf16[1024,128]{1,0:T(8,128)(2,1)} %get-tuple-element.135.refs_1_, bf16[1024,128]{1,0:T(8,128)(2,1)} %get-tuple-element.136.refs_2_, ...), custom_call_target="tpu_custom_call" | custom-call | flops 2147483648 | bytes 8388608 | tf_op jit(solution)/shard_map/self_joined/pallas_call | solution.py:57
  244.7 2.6 collective-permute-done.16.got
  248.2 3.2 %self_sum_core.1 = (bf16[2,2,2,16,768]{4,3,2,1,0:T(8,128)(2,1)}, bf16[2,2,2,16,896]{4,3,2,1,0:T(8,128)(2,1)}, f32[2,2,2,16,768]{4,3,2,1,0:T(8,128)}, f32[2,2,2,16,896]{4,3,2,1,0:T(8,128)}) custom-call(s32[5]{0:T(128)} %stack.275.bits.refs_0_, bf16[2,2,2,2,16,1664]{5,4,3,2,1,0:T(8,128)(2,1)} %bitcast.97, bf16[2,2,2,2,16,1664]{5,4,3,2,1,0:T(8,128)(2,1)} %copy-done.3), custom_call_target="tpu_custom_call" | custom-call | tf_op jit(solution)/shard_map/self_sum_core/pallas_call | solution.py:57
  253.2 5.7 %collective-permute-done.17.got_x = bf16[2,2,2,16,768]{4,3,2,1,0:T(8,128)(2,1)S(1)} collective-permute-done((bf16[2,2,2,16,768]{4,3,2,1,0:T(8,128)(2,1)}, bf16[2,2,2,16,768]{4,3,2,1,0:T(8,128)(2,1)S(1)}, u32[]{:S(2)}, u32[]{:S(2)}) %collective-permute-start.17) | collective-permute-done | bytes 196640 | tf_op jit(solution)/shard_map/ppermute | solution.py:482
  259.9 2.8 self_sum_plane.1
  265.0 3.7 %collective-permute-done.19.got_y = bf16[2,2,16,768]{3,2,1,0:T(8,128)(2,1)S(1)} collective-permute-done((bf16[2,2,16,768]{3,2,1,0:T(8,128)(2,1)}, bf16[2,2,16,768]{3,2,1,0:T(8,128)(2,1)S(1)}, u32[]{:S(2)}, u32[]{:S(2)}) %collective-permute-start.19) | collective-permute-done | bytes 98336 | tf_op jit(solution)/shard_map/ppermute | solution.py:482
  269.4 2.6 self_sum_line.1
  273.2 2.4 cross_sum_ends.1
  275.6 2.2 collective-permute-start.23
  278.4 2.3 self_sum_ends.1
  280.8 2.5 collective-permute-start.22
  283.3 8.1 %last_grads.1 = (f32[1024,512]{1,0:T(8,128)}, f32[1024,512]{1,0:T(8,128)}) custom-call(bf16[1024,128]{1,0:T(8,128)(2,1)} %get-tuple-element.115.refs_1_.refs_0_, bf16[1024,128]{1,0:T(8,128)(2,1)} %get-tuple-element.116.refs_2_.refs_1_, bf16[1024,128]{1,0:T(8,128)(2,1)} %get-tuple-element.117.refs_4_.refs_2_, ...), custom_call_target="tpu_custom_call" | custom-call | flops 3221225472 | bytes 12582912 | tf_op jit(solution)/shard_map/last_grads/pallas_call | solution.py:57
  (123 shorter events, 59.5 us)
Async XLA Ops:
  7.2 106.3 %all-gather.2.cloned.1.call-start = ((), (), s32[]{:S(2)}) async-start(), calls=%async_computation.2 | async-start | bytes 4325376 | tf_op jit(solution)/shard_map/all_gather | solution.py:691
  10.4 17.3 %copy-start.6 = (bf16[16,2304]{1,0:T(8,128)(2,1)S(1)}, bf16[16,2304]{1,0:T(8,128)(2,1)}, u32[]{:S(2)}) copy-start(bf16[16,2304]{1,0:T(8,128)(2,1)} %get-tuple-element.103) | copy-start | bytes 221188
  10.4 194.3 %reduce-scatter.3.cloned.1.call-start = ((), (), s32[]{:S(2)}) async-start(), calls=%async_computation.3 | async-start | bytes 5570560 | tf_op jit(solution)/shard_map/reduce_scatter | solution.py:753
  10.5 13.4 %collective-permute-start.5 = (bf16[16,2048]{1,0:T(8,128)(2,1)}, bf16[16,2048]{1,0:T(8,128)(2,1)S(1)}, u32[]{:S(2)}, u32[]{:S(2)}) collective-permute-start(bf16[16,2048]{1,0:T(8,128)(2,1)} %get-tuple-element.104), channel_id=1, source_target_pairs={{0,4},{1,5},{2,6},{3,7},{4,0},{5,1},{6,2},{7,3},{8,12},{9,13},{10,... | collective-permute-start | bytes 196616 | tf_op jit(solution)/shard_map/ppermute | solution.py:482
  14.6 13.1 %collective-permute-start = (bf16[16,2304]{1,0:T(8,128)(2,1)}, bf16[16,2304]{1,0:T(8,128)(2,1)S(1)}, u32[]{:S(2)}, u32[]{:S(2)}) collective-permute-start(bf16[16,2304]{1,0:T(8,128)(2,1)} %get-tuple-element.103), channel_id=1, source_target_pairs={{0,4},{1,5},{2,6},{3,7},{4,0},{5,1},{6,2},{7,3},{8,12},{9,13},{10,... | collective-permute-start | bytes 221192 | tf_op jit(solution)/shard_map/ppermute | solution.py:482
  24.8 7.2 %collective-permute-start.6 = (bf16[2,16,2048]{2,1,0:T(8,128)(2,1)S(1)}, bf16[2,16,2048]{2,1,0:T(8,128)(2,1)S(1)}, u32[]{:S(2)}, u32[]{:S(2)}) collective-permute-start(bf16[2,16,2048]{2,1,0:T(8,128)(2,1)S(1)} %maximum_select_fusion.16), channel_id=1, source_target_pairs={{0,2},{1,3},{2,0},{3,1},{4,6},{5,7},{6,4},{7,5},{8,10},{9,11},{10,... | collective-permute-start | bytes 393224 | tf_op jit(solution)/shard_map/ppermute | solution.py:482
  27.7 7.5 %collective-permute-start.1 = (bf16[2,16,2304]{2,1,0:T(8,128)(2,1)S(1)}, bf16[2,16,2304]{2,1,0:T(8,128)(2,1)S(1)}, u32[]{:S(2)}, u32[]{:S(2)}) collective-permute-start(bf16[2,16,2304]{2,1,0:T(8,128)(2,1)S(1)} %maximum_select_fusion.14), channel_id=1, source_target_pairs={{0,2},{1,3},{2,0},{3,1},{4,6},{5,7},{6,4},{7,5},{8,10},{9,11},{10,... | collective-permute-start | bytes 442376 | tf_op jit(solution)/shard_map/ppermute | solution.py:482
  32.1 6.4 %collective-permute-start.7 = (bf16[2,2,16,2048]{3,2,0,1:T(8,128)(2,1)S(1)}, bf16[2,2,16,2048]{3,2,0,1:T(8,128)(2,1)S(1)}, u32[]{:S(2)}, u32[]{:S(2)}) collective-permute-start(bf16[2,2,16,2048]{3,2,0,1:T(8,128)(2,1)S(1)} %maximum_select_fusion.12), channel_id=1, source_target_pairs={{0,16},{1,17},{2,18},{3,19},{4,20},{5,21},{6,22},{7,23},{8,24},{9,... | collective-permute-start | bytes 786440 | tf_op jit(solution)/shard_map/ppermute | solution.py:482
  35.2 12.9 %collective-permute-start.2 = (bf16[2,2,16,2304]{3,2,0,1:T(8,128)(2,1)S(1)}, bf16[2,2,16,2304]{3,2,0,1:T(8,128)(2,1)S(1)}, u32[]{:S(2)}, u32[]{:S(2)}) collective-permute-start(bf16[2,2,16,2304]{3,2,0,1:T(8,128)(2,1)S(1)} %maximum_select_fusion.10), channel_id=1, source_target_pairs={{0,8},{1,9},{2,10},{3,11},{4,12},{5,13},{6,14},{7,15},{8,0},{9,1},... | collective-permute-start | bytes 884744 | tf_op jit(solution)/shard_map/ppermute | solution.py:482
  38.6 19.4 %collective-permute-start.8 = (bf16[2,2,2,16,2048]{4,3,1,2,0:T(8,128)(2,1)S(1)}, bf16[2,2,2,16,2048]{4,3,1,2,0:T(8,128)(2,1)S(1)}, u32[]{:S(2)}, u32[]{:S(2)}) collective-permute-start(bf16[2,2,2,16,2048]{4,3,1,2,0:T(8,128)(2,1)S(1)} %maximum_select_fusion.8), channel_id=1, source_target_pairs={{0,8},{1,9},{2,10},{3,11},{4,12},{5,13},{6,14},{7,15},{8,0},{9,1},... | collective-permute-start | bytes 1572872 | tf_op jit(solution)/shard_map/ppermute | solution.py:482
  48.2 10.0 %collective-permute-start.3 = (bf16[2,2,2,16,2304]{4,3,1,2,0:T(8,128)(2,1)S(1)}, bf16[2,2,2,16,2304]{4,3,1,2,0:T(8,128)(2,1)S(1)}, u32[]{:S(2)}, u32[]{:S(2)}) collective-permute-start(bf16[2,2,2,16,2304]{4,3,1,2,0:T(8,128)(2,1)S(1)} %maximum_select_fusion.6), channel_id=1, source_target_pairs={{0,16},{1,17},{2,18},{3,19},{4,20},{5,21},{6,22},{7,23},{8,24},{9,... | collective-permute-start | bytes 1769480 | tf_op jit(solution)/shard_map/ppermute | solution.py:482
  58.1 2.7 collective-permute-start.9
  58.4 4.2 %collective-permute-start.4 = (bf16[2,2,2,2,16,2304]{5,4,2,3,1,0:T(8,128)(2,1)S(1)}, bf16[2,2,2,2,16,2304]{5,4,2,3,1,0:T(8,128)(2,1)S(1)}, u32[]{:S(2)}, u32[]{:S(2)}) collective-permute-start(bf16[2,2,2,2,16,2304]{5,4,2,3,1,0:T(8,128)(2,1)S(1)} %maximum_select_fusion.2), channel_id=1, source_target_pairs={{0,1},{1,0},{2,3},{3,2},{4,5},{5,4},{6,7},{7,6},{8,9},{9,8},{10,11... | collective-permute-start | bytes 3538952 | tf_op jit(solution)/shard_map/ppermute | solution.py:482
  143.8 152.1 %reduce-scatter.5.cloned.1.call-start = ((), (), s32[]{:S(2)}) async-start(), calls=%async_computation.4 | async-start | bytes 1253376 | tf_op jit(solution)/shard_map/reduce_scatter | solution.py:754
  189.9 7.0 %collective-permute-start.10 = (bf16[2,2,2,2,16,2688]{5,4,3,2,1,0:T(8,128)(2,1)}, bf16[2,2,2,2,16,2688]{5,4,3,2,1,0:T(8,128)(2,1)S(1)}, u32[]{:S(2)}, u32[]{:S(2)}) collective-permute-start(bf16[2,2,2,2,16,2688]{5,4,3,2,1,0:T(8,128)(2,1)} %bitcast.113), channel_id=1, source_target_pairs={{0,1},{1,0},{2,3},{3,2},{4,5},{5,4},{6,7},{7,6},{8,9},{9,8},{10,11... | collective-permute-start | bytes 4128776 | tf_op jit(solution)/shard_map/ppermute | solution.py:482
  196.8 1.1 copy-start
  201.8 11.1 %collective-permute-start.11 = (bf16[2,2,2,16,1408]{4,3,2,1,0:T(8,128)(2,1)}, bf16[2,2,2,16,1408]{4,3,2,1,0:T(8,128)(2,1)S(1)}, u32[]{:S(2)}, u32[]{:S(2)}) collective-permute-start(bf16[2,2,2,16,1408]{4,3,2,1,0:T(8,128)(2,1)} %get-tuple-element.143), channel_id=1, source_target_pairs={{0,8},{1,9},{2,10},{3,11},{4,12},{5,13},{6,14},{7,15},{8,0},{9,1},... | collective-permute-start | bytes 1081352 | tf_op jit(solution)/shard_map/ppermute | solution.py:482
  203.3 9.6 %collective-permute-start.12 = (bf16[2,2,2,16,1280]{4,3,2,1,0:T(8,128)(2,1)}, bf16[2,2,2,16,1280]{4,3,2,1,0:T(8,128)(2,1)S(1)}, u32[]{:S(2)}, u32[]{:S(2)}) collective-permute-start(bf16[2,2,2,16,1280]{4,3,2,1,0:T(8,128)(2,1)} %get-tuple-element.144), channel_id=1, source_target_pairs={{0,16},{1,17},{2,18},{3,19},{4,20},{5,21},{6,22},{7,23},{8,24},{9,... | collective-permute-start | bytes 983048 | tf_op jit(solution)/shard_map/ppermute | solution.py:482
  212.9 0.7 copy-start.2
  212.9 0.8 copy-start.1
  217.0 9.2 %collective-permute-start.13 = (bf16[2,2,16,1408]{3,2,1,0:T(8,128)(2,1)}, bf16[2,2,16,1408]{3,2,1,0:T(8,128)(2,1)S(1)}, u32[]{:S(2)}, u32[]{:S(2)}) collective-permute-start(bf16[2,2,16,1408]{3,2,1,0:T(8,128)(2,1)} %get-tuple-element.150), channel_id=1, source_target_pairs={{0,16},{1,17},{2,18},{3,19},{4,20},{5,21},{6,22},{7,23},{8,24},{9,... | collective-permute-start | bytes 540680 | tf_op jit(solution)/shard_map/ppermute | solution.py:482
  218.8 7.5 %collective-permute-start.14 = (bf16[2,2,16,1280]{3,2,1,0:T(8,128)(2,1)}, bf16[2,2,16,1280]{3,2,1,0:T(8,128)(2,1)S(1)}, u32[]{:S(2)}, u32[]{:S(2)}) collective-permute-start(bf16[2,2,16,1280]{3,2,1,0:T(8,128)(2,1)} %get-tuple-element.151), channel_id=1, source_target_pairs={{0,8},{1,9},{2,10},{3,11},{4,12},{5,13},{6,14},{7,15},{8,0},{9,1},... | collective-permute-start | bytes 491528 | tf_op jit(solution)/shard_map/ppermute | solution.py:482
  229.7 7.3 %collective-permute-start.15 = (bf16[2,16,2688]{2,1,0:T(8,128)(2,1)}, bf16[2,16,2688]{2,1,0:T(8,128)(2,1)S(1)}, u32[]{:S(2)}, u32[]{:S(2)}) collective-permute-start(bf16[2,16,2688]{2,1,0:T(8,128)(2,1)} %get-tuple-element.157), channel_id=1, source_target_pairs={{0,2},{1,3},{2,0},{3,1},{4,6},{5,7},{6,4},{7,5},{8,10},{9,11},{10,... | collective-permute-start | bytes 516104 | tf_op jit(solution)/shard_map/ppermute | solution.py:482
  244.7 2.6 collective-permute-start.16
  247.3 0.9 copy-start.3
  251.4 7.9 %collective-permute-start.18 = (bf16[2,2,2,16,896]{4,3,2,1,0:T(8,128)(2,1)}, bf16[2,2,2,16,896]{4,3,2,1,0:T(8,128)(2,1)S(1)}, u32[]{:S(2)}, u32[]{:S(2)}) collective-permute-start(bf16[2,2,2,16,896]{4,3,2,1,0:T(8,128)(2,1)} %get-tuple-element.167), channel_id=1, source_target_pairs={{0,16},{1,17},{2,18},{3,19},{4,20},{5,21},{6,22},{7,23},{8,24},{9,... | collective-permute-start | bytes 688136 | tf_op jit(solution)/shard_map/ppermute | solution.py:482
  252.0 6.9 %collective-permute-start.17 = (bf16[2,2,2,16,768]{4,3,2,1,0:T(8,128)(2,1)}, bf16[2,2,2,16,768]{4,3,2,1,0:T(8,128)(2,1)S(1)}, u32[]{:S(2)}, u32[]{:S(2)}) collective-permute-start(bf16[2,2,2,16,768]{4,3,2,1,0:T(8,128)(2,1)} %get-tuple-element.165), channel_id=1, source_target_pairs={{0,8},{1,9},{2,10},{3,11},{4,12},{5,13},{6,14},{7,15},{8,0},{9,1},... | collective-permute-start | bytes 589832 | tf_op jit(solution)/shard_map/ppermute | solution.py:482
  262.8 6.0 %collective-permute-start.20 = (bf16[2,2,16,896]{3,2,1,0:T(8,128)(2,1)}, bf16[2,2,16,896]{3,2,1,0:T(8,128)(2,1)S(1)}, u32[]{:S(2)}, u32[]{:S(2)}) collective-permute-start(bf16[2,2,16,896]{3,2,1,0:T(8,128)(2,1)} %get-tuple-element.171), channel_id=1, source_target_pairs={{0,8},{1,9},{2,10},{3,11},{4,12},{5,13},{6,14},{7,15},{8,0},{9,1},... | collective-permute-start | bytes 344072 | tf_op jit(solution)/shard_map/ppermute | solution.py:482
  263.9 4.8 %collective-permute-start.19 = (bf16[2,2,16,768]{3,2,1,0:T(8,128)(2,1)}, bf16[2,2,16,768]{3,2,1,0:T(8,128)(2,1)S(1)}, u32[]{:S(2)}, u32[]{:S(2)}) collective-permute-start(bf16[2,2,16,768]{3,2,1,0:T(8,128)(2,1)} %get-tuple-element.169), channel_id=1, source_target_pairs={{0,16},{1,17},{2,18},{3,19},{4,20},{5,21},{6,22},{7,23},{8,24},{9,... | collective-permute-start | bytes 294920 | tf_op jit(solution)/shard_map/ppermute | solution.py:482
  272.0 5.8 %collective-permute-start.21 = (bf16[2,16,1664]{2,1,0:T(8,128)(2,1)}, bf16[2,16,1664]{2,1,0:T(8,128)(2,1)S(1)}, u32[]{:S(2)}, u32[]{:S(2)}) collective-permute-start(bf16[2,16,1664]{2,1,0:T(8,128)(2,1)} %get-tuple-element.173), channel_id=1, source_target_pairs={{0,2},{1,3},{2,0},{3,1},{4,6},{5,7},{6,4},{7,5},{8,10},{9,11},{10,... | collective-permute-start | bytes 319496 | tf_op jit(solution)/shard_map/ppermute | solution.py:482
  275.6 15.8 %collective-permute-start.23 = (bf16[16,2688]{1,0:T(8,128)(2,1)}, bf16[16,2688]{1,0:T(8,128)(2,1)S(1)}, u32[]{:S(2)}, u32[]{:S(2)}) collective-permute-start(bf16[16,2688]{1,0:T(8,128)(2,1)} %get-tuple-element.178), channel_id=1, source_target_pairs={{0,4},{1,5},{2,6},{3,7},{4,0},{5,1},{6,2},{7,3},{8,12},{9,13},{10,... | collective-permute-start | bytes 258056 | tf_op jit(solution)/shard_map/ppermute | solution.py:482
  280.8 12.9 %collective-permute-start.22 = (bf16[16,1664]{1,0:T(8,128)(2,1)}, bf16[16,1664]{1,0:T(8,128)(2,1)S(1)}, u32[]{:S(2)}, u32[]{:S(2)}) collective-permute-start(bf16[16,1664]{1,0:T(8,128)(2,1)} %get-tuple-element.175), channel_id=1, source_target_pairs={{0,4},{1,5},{2,6},{3,7},{4,0},{5,1},{6,2},{7,3},{8,12},{9,13},{10,... | collective-permute-start | bytes 159752 | tf_op jit(solution)/shard_map/ppermute | solution.py:482
  (10 other events, 6.6 us)
Sparse Core Ops, SparseCore 0:
  11.6 67.9 all-gather.1
  143.9 55.7 reduce-scatter.2
  204.9 32.4 reduce-scatter.4
